TPU v7x, 32 devices: a whole 2x2x4 slice. The times are simulated.
32 devices in a mesh: ctx: 8 (over z, y), tp: 4 (over x, core).
Axes of the slice: x: 2, y: 2, z: 4, core: 2. Of those that a mesh axis runs over, the one named last changes fastest.
Arguments:
- query: bfloat16 [2048, 4096], P('ctx', 'tp'), may hold values from -96 to 96
- key: bfloat16 [2048, 4096], P('ctx', 'tp'), may hold values from -4 to 4
- value: bfloat16 [2048, 4096], P('ctx', 'tp'), may hold values from -6 to 6
- xin: bfloat16 [2048, 4096], P('ctx', 'tp'), may hold values from -1 to 8
- gate_z: bfloat16 [2048, 4096], P('ctx', 'tp'), may hold values from -6 to 6
- w_bc: bfloat16 [4096, 32], P('tp'), may hold values from -1 to 1
- dt_low: bfloat16 [2048, 256], P('ctx'), may hold values from -4 to 9
- dt_proj: bfloat16 [256, 4096], P(None, 'tp'), may hold values from -3 to 3
- dt_bias: float32 [4096], P('tp'), may hold values from -20 to 0
- a_rate: float32 [16, 4096], P(None, 'tp'), may hold values from 1 to 16
- skip: float32 [4096], P('tp'), may hold values from 0.2 to 2
Outputs:
- attended: bfloat16 [2048, 4096], P('ctx', 'tp')
- mixed: bfloat16 [2048, 4096], P('ctx', 'tp')
All inputs are finite; a program needn't handle non-finite values.
Results may differ from a plain program's by a relative error of at most 0.0085.
Values may be sent and summed in bfloat16 or wider, within the bound.
A program may use at most 128 MiB of HBM per device.

v0:
```python
import jax
import jax.numpy as jnp
from jax import lax
from jax.sharding import PartitionSpec as P

HD = 128
WINDOW = 2048
NS = 16


def passed_along(block, axis, distance):
    devices = range(lax.axis_size(axis))
    route = [(i - distance, i) for i in devices if i - distance in devices]
    return lax.ppermute(block, axis, route)


def entering(shard, axis, combine, identity):
    peers, here = (lax.axis_size(axis), lax.axis_index(axis))
    everything = jax.tree.map(lambda part: lax.all_gather(part, axis), shard)
    start = jax.tree.map(
        lambda part, zero: jnp.broadcast_to(jnp.asarray(zero, part.dtype), part.shape),
        shard,
        identity,
    )

    def step(k, before):
        reached = k < here
        new = combine(before, jax.tree.map(lambda part: part[k], everything))
        return jax.tree.map(lambda a, b: jnp.where(reached, a, b), new, before)

    return lax.fori_loop(0, peers, step, start)


def combine_states(earlier, later):
    return (earlier[0] * later[0], later[0] * earlier[1] + later[1])


def sweep_states(start_state, decay_rates, step_sizes, driven, b_rows, c_rows):
    tok_rows, channels = step_sizes.shape
    length = 32
    blocks = tok_rows // length
    inputs = (
        step_sizes.reshape(blocks, length, channels),
        driven.reshape(blocks, length, channels),
        b_rows.reshape(blocks, length, b_rows.shape[1]),
        c_rows.reshape(blocks, length, c_rows.shape[1]),
    )

    def advance(carried, block_in):
        sizes_block, drive_block, b_block, c_block = block_in
        outputs = []
        for offset in range(length):
            carried = (
                jnp.exp(-sizes_block[offset][None, :] * decay_rates) * carried
                + drive_block[offset][None, :] * b_block[offset][:, None]
            )
            outputs.append(jnp.sum(c_block[offset][:, None] * carried, axis=0))
        return (carried, jnp.stack(outputs))

    last_state, produced = lax.scan(advance, start_state, inputs)
    return (last_state, produced.reshape(tok_rows, channels))


def window_attention(query, pieces, place, reach):
    tok_rows = query.shape[0]
    ordered = jnp.concatenate(pieces[::-1], axis=1)
    key_pos = (place - reach) * tok_rows + jnp.arange(ordered.shape[1], dtype=jnp.int32)
    query_pos = place * tok_rows + jnp.arange(tok_rows, dtype=jnp.int32)
    allowed = (
        (key_pos[None, :] <= query_pos[:, None])
        & (key_pos[None, :] > query_pos[:, None] - WINDOW)
        & (key_pos[None, :] >= 0)
    )
    scale = HD ** (-0.5)
    heads_dev = query.shape[1] // HD
    results = []
    for head_num in range(heads_dev):
        column = slice(head_num * HD, (head_num + 1) * HD)
        scores = (
            lax.dot_general(
                query[:, column],
                ordered[0][:, column],
                (((1,), (1,)), ((), ())),
                preferred_element_type=jnp.float32,
            )
            * scale
        )
        masked = jnp.where(allowed, scores, -jnp.inf)
        row_max = jnp.max(masked, axis=1, keepdims=True)
        unscaled = jnp.where(allowed, jnp.exp(scores - row_max), 0.0)
        row_sum = jnp.sum(unscaled, axis=1, keepdims=True)
        probs = (unscaled / row_sum).astype(jnp.bfloat16)
        results.append(
            jnp.dot(probs, ordered[1][:, column], preferred_element_type=jnp.float32).astype(
                jnp.bfloat16
            )
        )
    return jnp.concatenate(results, axis=1)


def shards(query, key, value, xin, gate_z, w_bc, dt_low, dt_proj, dt_bias, a_rate, skip):
    tok_rows = query.shape[0]
    place = lax.axis_index("ctx")
    stacked = jnp.stack([key, value])
    reach = WINDOW // tok_rows
    pieces = [stacked]
    for distance in range(1, reach + 1):
        pieces.append(passed_along(stacked, "ctx", distance))
    partial_bc = jnp.dot(xin, w_bc, preferred_element_type=jnp.float32)
    summed_bc = lax.psum(partial_bc, "tp")
    b_rows = summed_bc[:, :NS]
    c_rows = summed_bc[:, NS:]
    step_sizes = jax.nn.softplus(
        jnp.dot(dt_low, dt_proj, preferred_element_type=jnp.float32) + dt_bias[None, :]
    )
    inputs_float = xin.astype(jnp.float32)
    driven = step_sizes * inputs_float
    zero_state = jnp.zeros((NS, step_sizes.shape[1]), jnp.float32)
    local_end, local_out = sweep_states(zero_state, a_rate, step_sizes, driven, b_rows, c_rows)
    lower = (jnp.arange(tok_rows)[:, None] >= jnp.arange(tok_rows)[None, :]).astype(jnp.float32)
    running = jnp.dot(lower, step_sizes, precision=lax.Precision.HIGHEST)
    through = running[-1]
    decay_all = jnp.exp(-a_rate * through[None, :])
    prefix = entering(
        (decay_all, local_end),
        "ctx",
        combine_states,
        (jnp.ones_like(decay_all), jnp.zeros_like(local_end)),
    )
    incoming = prefix[1]
    attended = window_attention(query, pieces, place, reach)
    outputs = local_out
    for state_number in range(NS):
        outputs = (
            outputs
            + c_rows[:, state_number : state_number + 1]
            * jnp.exp(-running * a_rate[state_number][None, :])
            * incoming[state_number][None, :]
        )
    mixed = (
        (outputs + skip[None, :] * inputs_float) * jax.nn.silu(gate_z.astype(jnp.float32))
    ).astype(jnp.bfloat16)
    return (attended, mixed)


def solution(mesh):
    in_specs = (
        P("ctx", "tp"),
        P("ctx", "tp"),
        P("ctx", "tp"),
        P("ctx", "tp"),
        P("ctx", "tp"),
        P("tp", None),
        P("ctx", None),
        P(None, "tp"),
        P("tp"),
        P(None, "tp"),
        P("tp"),
    )
    out_specs = (P("ctx", "tp"), P("ctx", "tp"))
    return jax.shard_map(shards, mesh=mesh, in_specs=in_specs, out_specs=out_specs, check_vma=False)
```

profile of v0, /device:TPU:18, one launch (start us, length us, event | category | flops | bytes accessed | tf_op | source)
XLA Modules:
  0.0 311.2 jit_solution(268010740196250464)
XLA Ops:
  0.7 2.4 pad_maximum_fusion
  3.0 1.6 collective-permute-start
  4.7 1.6 collective-permute-start.1
  6.3 1.7 collective-permute-start.2
  8.0 1.6 collective-permute-start.3
  12.3 10.4 %psum.7 = f32[256,32]{0,1:T(8,128)S(1)} all-reduce(f32[256,32]{0,1:T(8,128)S(1)} %fusion.196), channel_id=1, replica_groups=mesh['ctx'=8,'tp'=4] {'tp'}, use_global_device_ids=true, to_apply=%region_16.17 | all-reduce | flops 8192 | bytes 65536 | tf_op jit(solution)/shard_map/psum | solution.py:110
  22.9 1.8 convert_multiply_fusion.2
  25.4 102.4 %while.27 = (s32[]{:T(128)}, f32[16,1024]{1,0:T(8,128)S(1)}, f32[8,32,1024]{2,1,0:T(8,128)}, f32[8,32,1024]{2,1,0:T(8,128)S(1)}, f32[16,1024]{1,0:T(8,128)S(1)},...) while((s32[]{:T(128)}, f32[16,1024]{1,0:T(8,128)S(1)}, ...), condition=%wide.region_50.51_spmd.clone, body=%wide.region_17.50_spmd.clone.sunk | while | flops 4685858 | bytes 3613532 | solution.py:60
  41.7 1.4 constant_dynamic-slice_fusion.130
  127.9 35.4 %all-gather = f32[128,1024]{1,0:T(8,128)S(1)} all-gather(f32[16,1024]{1,0:T(8,128)S(1)} %multiply_exponential_fusion), channel_id=2, replica_groups=mesh['ctx'=8,'tp'=4] {'ctx'}, dimensions={0}, use_global_device_ids=true | all-gather | bytes 589824 | tf_op jit(solution)/shard_map/all_gather | solution.py:19
  163.3 38.3 %all-gather.1 = f32[128,1024]{1,0:T(8,128)S(1)} all-gather(f32[16,1024]{1,0:T(8,128)S(1)} %get-tuple-element.140), channel_id=3, replica_groups=mesh['ctx'=8,'tp'=4] {'ctx'}, dimensions={0}, use_global_device_ids=true | all-gather | bytes 589824 | tf_op jit(solution)/shard_map/all_gather | solution.py:19
  202.1 6.1 %collective-permute-start.5 = (bf16[2,256,1024]{2,1,0:T(8,128)(2,1)}, bf16[2,256,1024]{2,1,0:T(8,128)(2,1)S(1)}, u32[]{:S(2)}, u32[]{:S(2)}) collective-permute-start(bf16[2,256,1024]{2,1,0:T(8,128)(2,1)} %pad_maximum_fusion), channel_id=1, source_target_pairs={{0,12},{4,16},{8,20},{12,24},{16,28},{1,13},{5,17},{9,21},{13,25},... | collective-permute-start | bytes 3145736 | tf_op jit(solution)/shard_map/ppermute | solution.py:14
  208.3 6.1 %fusion.140 = bf16[256,1024]{1,0:T(8,128)(2,1)} fusion(bf16[256,1024]{1,0:T(8,128)(2,1)S(1)} %copy-done.5, bf16[256,1024]{1,0:T(8,128)(2,1)} %param.19, f32[8,32,1024]{2,1,0:T(8,128)} %get-tuple-element.139, f32[256,1024]{1,0:T(8,128)S(1)} %fusion.175, f32[1024]{0:T(1024)S(1)} %copy-done.17, f32[1024]{0:T(1024)S(1)} %bitcast.739, f32[1024]{0:T(1024)S(1)} %bitcast.723, ...), kind=kLoop, calls=%fused_computation.376 | loop fusion | flops 19660800 | bytes 3821568 | tf_op jit(solution)/shard_map/convert_element_type | solution.py:142
  214.4 7.1 %collective-permute-start.6 = (bf16[2,256,1024]{2,1,0:T(8,128)(2,1)}, bf16[2,256,1024]{2,1,0:T(8,128)(2,1)S(1)}, u32[]{:S(2)}, u32[]{:S(2)}) collective-permute-start(bf16[2,256,1024]{2,1,0:T(8,128)(2,1)} %pad_maximum_fusion), channel_id=1, source_target_pairs={{0,8},{4,12},{8,16},{12,20},{16,24},{20,28},{1,9},{5,13},{9,17},{1... | collective-permute-start | bytes 3145736 | tf_op jit(solution)/shard_map/ppermute | solution.py:14
  221.5 2.1 collective-permute-start.7
  223.6 2.3 constant_dynamic-update-slice_fusion.8
  225.9 2.3 constant_dynamic-update-slice_fusion.7
  228.2 2.3 constant_dynamic-update-slice_fusion.6
  230.5 2.3 constant_dynamic-update-slice_fusion.5
  232.8 2.3 constant_dynamic-update-slice_fusion.4
  237.2 42.7 %collective-permute-done.7 = bf16[2,256,1024]{2,1,0:T(8,128)(2,1)S(1)} collective-permute-done((bf16[2,256,1024]{2,1,0:T(8,128)(2,1)}, bf16[2,256,1024]{2,1,0:T(8,128)(2,1)S(1)}, u32[]{:S(2)}, u32[]{:S(2)}) %collective-permute-start.7) | collective-permute-done | bytes 1048608 | tf_op jit(solution)/shard_map/ppermute | solution.py:14
  282.0 7.2 %slice_bitcast_fusion = (bf16[2304,1024]{1,0:T(8,128)(2,1)}, bf16[2304,1024]{1,0:T(8,128)(2,1)S(1)}) fusion(bf16[2,2304,1024]{2,1,0:T(8,128)(2,1)} %constant_dynamic-update-slice_fusion), kind=kLoop, calls=%fused_computation.293 | loop fusion | bytes 18874368 | tf_op jit(solution)/shard_map/squeeze | solution.py:94
  293.1 2.5 fusion.113
  297.0 4.0 %fusion.112 = (f32[256]{0:T(256)S(1)}, f32[256]{0:T(256)S(1)}, f32[256]{0:T(256)S(1)}, f32[256]{0:T(256)S(1)}, f32[256]{0:T(256)S(1)}, /*index=5*/f32[256]{0:T(256)S(1)}) fusion(f32[256,2304]{0,1:T(8,128)S(1)} %fusion.104, f32[256]{0:T(256)S(1)} %get-tuple-element.235, pred[2304]{0:T(1024)(128)(4,1)S(1)} %broadcast_compare_fusion, ...), kind=kLoop, calls=%fused_computation.343 | loop fusion | flops 12974592 | bytes 14181632 | tf_op jit(solution)/shard_map/reduce_sum | solution.py:91
  (357 shorter events, 123.1 us)
Async XLA Ops:
  0.6 22.3 %copy-start = (bf16[256,1024]{1,0:T(8,128)(2,1)S(1)}, bf16[256,1024]{1,0:T(8,128)(2,1)}, u32[]{:S(2)}) copy-start(bf16[256,1024]{1,0:T(8,128)(2,1)} %param.22) | copy-start | bytes 1572868
  0.6 22.3 %copy-start.4 = (bf16[256,1024]{1,0:T(8,128)(2,1)S(1)}, bf16[256,1024]{1,0:T(8,128)(2,1)}, u32[]{:S(2)}) copy-start(bf16[256,1024]{1,0:T(8,128)(2,1)} %param.18) | copy-start | bytes 1572868
  0.7 22.3 %copy-start.16 = (f32[1024]{0:T(1024)S(1)}, f32[1024]{0:T(1024)}, u32[]{:S(2)}) copy-start(f32[1024]{0:T(1024)} %param.23) | copy-start | bytes 12292
  0.7 22.3 %copy-start.15 = (bf16[256,256]{1,0:T(8,128)(2,1)S(1)}, bf16[256,256]{1,0:T(8,128)(2,1)}, u32[]{:S(2)}) copy-start(bf16[256,256]{1,0:T(8,128)(2,1)} %param.21) | copy-start | bytes 393220
  3.0 199.0 %collective-permute-start = (bf16[2,256,1024]{2,1,0:T(8,128)(2,1)}, bf16[2,256,1024]{2,1,0:T(8,128)(2,1)}, u32[]{:S(2)}, u32[]{:S(2)}) collective-permute-start(bf16[2,256,1024]{2,1,0:T(8,128)(2,1)} %pad_maximum_fusion), channel_id=1, source_target_pairs={} | collective-permute-start | bytes 3145736 | tf_op jit(solution)/shard_map/ppermute | solution.py:14
  4.7 209.7 %collective-permute-start.1 = (bf16[2,256,1024]{2,1,0:T(8,128)(2,1)}, bf16[2,256,1024]{2,1,0:T(8,128)(2,1)}, u32[]{:S(2)}, u32[]{:S(2)}) collective-permute-start(bf16[2,256,1024]{2,1,0:T(8,128)(2,1)} %pad_maximum_fusion), channel_id=1, source_target_pairs={{0,28},{1,29},{2,30},{3,31}} | collective-permute-start | bytes 3145736 | tf_op jit(solution)/shard_map/ppermute | solution.py:14
  6.3 215.2 %collective-permute-start.2 = (bf16[2,256,1024]{2,1,0:T(8,128)(2,1)}, bf16[2,256,1024]{2,1,0:T(8,128)(2,1)}, u32[]{:S(2)}, u32[]{:S(2)}) collective-permute-start(bf16[2,256,1024]{2,1,0:T(8,128)(2,1)} %pad_maximum_fusion), channel_id=1, source_target_pairs={{0,24},{4,28},{1,25},{5,29},{2,26},{6,30},{3,27},{7,31}} | collective-permute-start | bytes 3145736 | tf_op jit(solution)/shard_map/ppermute | solution.py:14
  8.0 222.5 %collective-permute-start.3 = (bf16[2,256,1024]{2,1,0:T(8,128)(2,1)}, bf16[2,256,1024]{2,1,0:T(8,128)(2,1)}, u32[]{:S(2)}, u32[]{:S(2)}) collective-permute-start(bf16[2,256,1024]{2,1,0:T(8,128)(2,1)} %pad_maximum_fusion), channel_id=1, source_target_pairs={{0,20},{4,24},{8,28},{1,21},{5,25},{9,29},{2,22},{6,26},{10,30},{3... | collective-permute-start | bytes 3145736 | tf_op jit(solution)/shard_map/ppermute | solution.py:14
  9.6 223.2 %collective-permute-start.4 = (bf16[2,256,1024]{2,1,0:T(8,128)(2,1)}, bf16[2,256,1024]{2,1,0:T(8,128)(2,1)}, u32[]{:S(2)}, u32[]{:S(2)}) collective-permute-start(bf16[2,256,1024]{2,1,0:T(8,128)(2,1)} %pad_maximum_fusion), channel_id=1, source_target_pairs={{0,16},{4,20},{8,24},{12,28},{1,17},{5,21},{9,25},{13,29},{2,18},{... | collective-permute-start | bytes 3145736 | tf_op jit(solution)/shard_map/ppermute | solution.py:14
  30.5 6.7 %copy-start.7 = (f32[16]{0:T(128)S(1)}, f32[16]{0:T(128)}, u32[]{:S(2)}) copy-start(f32[16]{0:T(128)} %get-tuple-element.885) | copy-start | bytes 196 | tf_op jit(solution)/shard_map/while
  30.5 6.7 %copy-start.8 = (f32[16]{0:T(128)S(1)}, f32[16]{0:T(128)}, u32[]{:S(2)}) copy-start(f32[16]{0:T(128)} %get-tuple-element.881) | copy-start | bytes 196 | tf_op jit(solution)/shard_map/while
  30.5 6.7 %copy-start.9 = (f32[16]{0:T(128)S(1)}, f32[16]{0:T(128)}, u32[]{:S(2)}) copy-start(f32[16]{0:T(128)} %get-tuple-element.883) | copy-start | bytes 196 | tf_op jit(solution)/shard_map/while
  30.5 6.7 %copy-start.10 = (f32[16]{0:T(128)S(1)}, f32[16]{0:T(128)}, u32[]{:S(2)}) copy-start(f32[16]{0:T(128)} %get-tuple-element.884) | copy-start | bytes 196 | tf_op jit(solution)/shard_map/while
  43.4 6.7 %copy-start.7 = (f32[16]{0:T(128)S(1)}, f32[16]{0:T(128)}, u32[]{:S(2)}) copy-start(f32[16]{0:T(128)} %get-tuple-element.885) | copy-start | bytes 196 | tf_op jit(solution)/shard_map/while
  43.4 6.7 %copy-start.8 = (f32[16]{0:T(128)S(1)}, f32[16]{0:T(128)}, u32[]{:S(2)}) copy-start(f32[16]{0:T(128)} %get-tuple-element.881) | copy-start | bytes 196 | tf_op jit(solution)/shard_map/while
  43.5 6.7 %copy-start.9 = (f32[16]{0:T(128)S(1)}, f32[16]{0:T(128)}, u32[]{:S(2)}) copy-start(f32[16]{0:T(128)} %get-tuple-element.883) | copy-start | bytes 196 | tf_op jit(solution)/shard_map/while
  127.8 80.4 %copy-start.5 = (bf16[256,1024]{1,0:T(8,128)(2,1)S(1)}, bf16[256,1024]{1,0:T(8,128)(2,1)}, u32[]{:S(2)}) copy-start(bf16[256,1024]{1,0:T(8,128)(2,1)} %param.18) | copy-start | bytes 1572868
  127.8 80.4 %copy-start.17 = (f32[1024]{0:T(1024)S(1)}, f32[1024]{0:T(1024)}, u32[]{:S(2)}) copy-start(f32[1024]{0:T(1024)} %param.25) | copy-start | bytes 12292
  202.1 33.0 %collective-permute-start.5 = (bf16[2,256,1024]{2,1,0:T(8,128)(2,1)}, bf16[2,256,1024]{2,1,0:T(8,128)(2,1)S(1)}, u32[]{:S(2)}, u32[]{:S(2)}) collective-permute-start(bf16[2,256,1024]{2,1,0:T(8,128)(2,1)} %pad_maximum_fusion), channel_id=1, source_target_pairs={{0,12},{4,16},{8,20},{12,24},{16,28},{1,13},{5,17},{9,21},{13,25},... | collective-permute-start | bytes 3145736 | tf_op jit(solution)/shard_map/ppermute | solution.py:14
  214.4 21.8 %collective-permute-start.6 = (bf16[2,256,1024]{2,1,0:T(8,128)(2,1)}, bf16[2,256,1024]{2,1,0:T(8,128)(2,1)S(1)}, u32[]{:S(2)}, u32[]{:S(2)}) collective-permute-start(bf16[2,256,1024]{2,1,0:T(8,128)(2,1)} %pad_maximum_fusion), channel_id=1, source_target_pairs={{0,8},{4,12},{8,16},{12,20},{16,24},{20,28},{1,9},{5,13},{9,17},{1... | collective-permute-start | bytes 3145736 | tf_op jit(solution)/shard_map/ppermute | solution.py:14
  221.5 58.4 %collective-permute-start.7 = (bf16[2,256,1024]{2,1,0:T(8,128)(2,1)}, bf16[2,256,1024]{2,1,0:T(8,128)(2,1)S(1)}, u32[]{:S(2)}, u32[]{:S(2)}) collective-permute-start(bf16[2,256,1024]{2,1,0:T(8,128)(2,1)} %pad_maximum_fusion), channel_id=1, source_target_pairs={{0,4},{4,8},{8,12},{12,16},{16,20},{20,24},{24,28},{1,5},{5,9},{9,... | collective-permute-start | bytes 3145736 | tf_op jit(solution)/shard_map/ppermute | solution.py:14
  236.1 44.8 %copy-start.2 = (bf16[256,1024]{1,0:T(8,128)(2,1)S(1)}, bf16[256,1024]{1,0:T(8,128)(2,1)}, u32[]{:S(2)}) copy-start(bf16[256,1024]{1,0:T(8,128)(2,1)} %param.17) | copy-start | bytes 1572868
  236.1 44.8 %copy-start.3 = (bf16[256,1024]{1,0:T(8,128)(2,1)S(1)}, bf16[256,1024]{1,0:T(8,128)(2,1)}, u32[]{:S(2)}) copy-start(bf16[256,1024]{1,0:T(8,128)(2,1)} %param.16) | copy-start | bytes 1572868
  282.0 7.2 %copy-start.6 = (bf16[256,1024]{1,0:T(8,128)(2,1)S(1)}, bf16[256,1024]{1,0:T(8,128)(2,1)}, u32[]{:S(2)}) copy-start(bf16[256,1024]{1,0:T(8,128)(2,1)} %param.15) | copy-start | bytes 1572868
  (60 other events, 383.3 us)
where the time goes:
time: 314 us; the launch traced here: 311 us
  blocking collectives  84.1 us (27%)
  other arithmetic  69.2 us (22%)
  local copies, waits for them, and re-layouts  68.5 us (22%)
  waiting for transfers between devices  42.7 us (14%)
  starting transfers between devices  23.2 us (7%)
  matrix products  20.7 us (7%)
    all_gather x2, blocking collectives, entering(): everything = jax.tree.map(lambda part: lax.all_gather(part, axis), shard)  73.7 us
    reduce_sum x72, other arithmetic, advance(): outputs.append(jnp.sum(c_block[offset][:, None] * carried, axis=0))  53.4 us
    ppermute x8, waiting for transfers between devices, passed_along(): return lax.ppermute(block, axis, route)  42.7 us
    ppermute x8, starting transfers between devices, passed_along(): return lax.ppermute(block, axis, route)  23.2 us
    slice x16, local copies, waits for them, and re-layouts, advance(): drive_block[offset][None, :] * b_block[offset][:, None]  20.7 us
    unnamed x35, local copies, waits for them, and re-layouts  15.9 us
    mul x16, local copies, waits for them, and re-layouts, advance(): drive_block[offset][None, :] * b_block[offset][:, None]  11.8 us
    dot_general x8, matrix products, window_attention(): jnp.dot(probs, ordered[1][:, column], preferred_element_type=jnp.float32)  10.5 us
  transfers between devices with their start and end apart: 8, of which 1 were waited for; matrix products, arithmetic and copies ran while one was open for 40% of the time, Pallas kernels for 0%

commit v1 on v0

v1 whole, which is shorter than its diff:
```python
import functools
import math

import jax
import jax.numpy as jnp
from jax import lax
from jax.experimental import pallas as pl
from jax.experimental.pallas import tpu as pltpu
from jax.sharding import PartitionSpec as P

HD = 128
WINDOW = 2048
NS = 16
LANES = 128
SUB = 8
LOG2E = math.log2(math.e)
RADIX = 8
VMEM = pl.BlockSpec(memory_space=pltpu.VMEM)
SMEM = pl.BlockSpec(memory_space=pltpu.SMEM)
PARAMS = pltpu.CompilerParams(vmem_limit_bytes=40 * 1024 * 1024)


def shifted(block, axis, distance):
    peers = lax.axis_size(axis)
    return lax.ppermute(block, axis, [(i, i + distance) for i in range(peers - distance)])


def rotated(block, axis, group, distance):
    peers = lax.axis_size(axis)
    route = [(i, i // group * group + (i % group + distance) % group) for i in range(peers)]
    return lax.ppermute(block, axis, route)


def head_at(group, distance):
    slot = lax.rem(lax.axis_index("ctx"), group)
    return lax.rem(slot + distance + group, group)


def pack_kernel(group, q_ref, k_ref, v_ref, *outs):
    for d in range(group):
        col = pl.ds(pl.multiple_of(head_at(group, d) * HD, HD), HD)
        for part, ref in enumerate((q_ref, k_ref, v_ref)):
            outs[d][part] = ref[:, col]


def pack(query, key, value, group):
    rows = query.shape[0]
    return pl.pallas_call(
        functools.partial(pack_kernel, group),
        out_shape=[jax.ShapeDtypeStruct((3, rows, HD), query.dtype)] * group,
        in_specs=[VMEM] * 3,
        out_specs=[VMEM] * group,
        compiler_params=PARAMS,
        cost_estimate=pl.CostEstimate(flops=0, bytes_accessed=6 * query.size * 2, transcendentals=0),
    )(query, key, value)


def unpack_kernel(group, *refs):
    out = refs[group]
    for d in range(group):
        col = pl.ds(pl.multiple_of(head_at(group, -d) * HD, HD), HD)
        out[:, col] = refs[d][...]


def unpack(blocks, group):
    rows = blocks[0].shape[0]
    return pl.pallas_call(
        functools.partial(unpack_kernel, group),
        out_shape=jax.ShapeDtypeStruct((rows, group * HD), blocks[0].dtype),
        in_specs=[VMEM] * group,
        out_specs=VMEM,
        compiler_params=PARAMS,
        cost_estimate=pl.CostEstimate(flops=0, bytes_accessed=4 * rows * group * HD, transcendentals=0),
    )(*blocks)


def attention_kernel(group, rows, with_prev, *refs):
    sets = 2 if with_prev else 1
    outs = refs[sets * group : (sets + 1) * group]
    q_s, k_s, v_s, o_s = refs[(sets + 1) * group :]
    base = group * rows if with_prev else 0
    for d in range(group):
        at = head_at(group, -d) * rows
        src = refs[d]
        q_s[pl.ds(pl.multiple_of(at, rows), rows), :] = src[0]
        k_s[pl.ds(pl.multiple_of(base + at, rows), rows), :] = src[1]
        v_s[pl.ds(pl.multiple_of(base + at, rows), rows), :] = src[2]
        if with_prev:
            old = refs[group + d]
            k_s[pl.ds(pl.multiple_of(at, rows), rows), :] = old[0]
            v_s[pl.ds(pl.multiple_of(at, rows), rows), :] = old[1]
    row = lax.broadcasted_iota(jnp.int32, (rows, rows), 0)
    col = lax.broadcasted_iota(jnp.int32, (rows, rows), 1)
    factor = HD**-0.5 * LOG2E
    for i in range(group):
        lo = i * rows if with_prev else 0
        hi = base + (i + 1) * rows
        q = q_s[i * rows : (i + 1) * rows, :]
        s = lax.dot_general(
            q, k_s[lo:hi, :], (((1,), (1,)), ((), ())), preferred_element_type=jnp.float32
        )
        last = jnp.where(col <= row, s[:, hi - lo - rows :], -jnp.inf)
        parts = [s[:, : hi - lo - rows], last] if hi - lo > rows else [last]
        if with_prev:
            held = lax.axis_index("ctx") >= group
            middle = s[:, rows : hi - lo - rows]
            first = jnp.where((col > row) & held, s[:, :rows], -jnp.inf)
            number = lax.broadcasted_iota(jnp.int32, middle.shape, 1) + (lo + rows)
            middle = jnp.where((number >= base) | held, middle, -jnp.inf)
            parts = [first, middle, last]
        s = jnp.concatenate(parts, axis=1) if len(parts) > 1 else parts[0]
        top = jnp.max(s, axis=1, keepdims=True)
        p = jnp.exp2((s - top) * factor)
        total = jnp.sum(p, axis=1, keepdims=True)
        o = jnp.dot(p.astype(jnp.bfloat16), v_s[lo:hi, :], preferred_element_type=jnp.float32)
        o_s[i * rows : (i + 1) * rows, :] = (o / total).astype(jnp.bfloat16)
    for d in range(group):
        at = head_at(group, d) * rows
        outs[d][...] = o_s[pl.ds(pl.multiple_of(at, rows), rows), :]


def attention(blocks, old, group):
    rows = blocks[0].shape[1]
    with_prev = old is not None
    length = group * rows
    keys = length * (2 if with_prev else 1)
    operands = list(blocks) + (list(old) if with_prev else [])
    bf16 = jnp.bfloat16
    return pl.pallas_call(
        functools.partial(attention_kernel, group, rows, with_prev),
        out_shape=[jax.ShapeDtypeStruct((rows, HD), bf16)] * group,
        in_specs=[VMEM] * len(operands),
        out_specs=[VMEM] * group,
        scratch_shapes=[
            pltpu.VMEM((length, HD), bf16),
            pltpu.VMEM((keys, HD), bf16),
            pltpu.VMEM((keys, HD), bf16),
            pltpu.VMEM((length, HD), bf16),
        ],
        compiler_params=PARAMS,
        cost_estimate=pl.CostEstimate(
            flops=2 * length * keys * HD,
            bytes_accessed=8 * length * HD,
            transcendentals=length * keys // 2,
        ),
    )(*operands)


def scan_kernel(delta_ref, x_ref, a_ref, bc_ref, y_ref, d_ref, end_ref, u_s):
    rows = delta_ref.shape[0]
    for c in range(SUB):
        cols = slice(c * LANES, (c + 1) * LANES)
        dt = delta_ref[:, cols]
        d_ref[pl.ds(c, rows, stride=SUB), :] = dt
        u_s[pl.ds(c, rows, stride=SUB), :] = dt * x_ref[:, cols].astype(jnp.float32)

    per = 4

    def step(block, carry):
        states, through = list(carry[:NS]), carry[NS]
        for k in range(per):
            t = block * per + k
            at = pl.ds(pl.multiple_of(t * SUB, SUB), SUB)
            dt, u = d_ref[at, :], u_s[at, :]
            through = through + dt
            sums = [None] * 4
            for n in range(NS):
                e = jnp.exp2(dt * a_ref[n * SUB : (n + 1) * SUB, :])
                states[n] = e * states[n] + u * bc_ref[t, n]
                term = states[n] * bc_ref[t, NS + n]
                sums[n % 4] = term if n < 4 else sums[n % 4] + term
            y_ref[at, :] = (sums[0] + sums[1]) + (sums[2] + sums[3])
        return (*states, through)

    zero = jnp.zeros((SUB, LANES), jnp.float32)
    ends = lax.fori_loop(0, rows // per, step, (zero,) * (NS + 1))
    for n in range(NS + 1):
        end_ref[n * SUB : (n + 1) * SUB, :] = ends[n]


def scan_block(delta, x, rate2, bc):
    rows, channels = delta.shape
    f32 = jnp.float32
    tiles = jax.ShapeDtypeStruct((rows * SUB, LANES), f32)
    return pl.pallas_call(
        scan_kernel,
        out_shape=[tiles, tiles, jax.ShapeDtypeStruct(((NS + 1) * SUB, LANES), f32)],
        in_specs=[VMEM, VMEM, VMEM, SMEM],
        out_specs=[VMEM] * 3,
        scratch_shapes=[pltpu.VMEM((rows * SUB, LANES), f32)],
        compiler_params=PARAMS,
        cost_estimate=pl.CostEstimate(
            flops=200 * rows * channels * NS,
            bytes_accessed=14 * rows * channels,
            transcendentals=rows * channels * NS,
        ),
    )(delta, x, rate2, bc)


def finish_kernel(count, *refs):
    ends = refs[:count]
    y_ref, d_ref, a_ref, bc_ref, x_ref, gate_ref, skip_ref, out_ref, y_s = refs[count:]
    rows = x_ref.shape[0]
    tile = [slice(n * SUB, (n + 1) * SUB) for n in range(NS + 1)]
    states = [jnp.zeros((SUB, LANES), jnp.float32)] * NS
    for end in ends:
        through = end[tile[NS], :]
        states = [
            jnp.exp2(through * a_ref[tile[n], :]) * states[n] + end[tile[n], :] for n in range(NS)
        ]
    per = 4

    def step(block, carry):
        held = list(carry)
        for k in range(per):
            t = block * per + k
            at = pl.ds(pl.multiple_of(t * SUB, SUB), SUB)
            dt = d_ref[at, :]
            sums = [y_ref[at, :], None, None, None]
            for n in range(NS):
                held[n] = jnp.exp2(dt * a_ref[tile[n], :]) * held[n]
                term = held[n] * bc_ref[t, NS + n]
                sums[n % 4] = term if sums[n % 4] is None else sums[n % 4] + term
            y_s[at, :] = (sums[0] + sums[1]) + (sums[2] + sums[3])
        return tuple(held)

    lax.fori_loop(0, rows // per, step, tuple(states))
    for c in range(SUB):
        cols = slice(c * LANES, (c + 1) * LANES)
        y = y_s[pl.ds(c, rows, stride=SUB), :] + skip_ref[:, cols] * x_ref[:, cols].astype(jnp.float32)
        g = gate_ref[:, cols].astype(jnp.float32)
        out_ref[:, cols] = (y * (g / (1.0 + jnp.exp(-g)))).astype(out_ref.dtype)


def finish(ends, y, d, rate2, bc, x, gate, skip):
    rows, channels = x.shape
    return pl.pallas_call(
        functools.partial(finish_kernel, len(ends)),
        out_shape=jax.ShapeDtypeStruct((rows, channels), jnp.bfloat16),
        in_specs=[VMEM] * len(ends) + [VMEM, VMEM, VMEM, SMEM, VMEM, VMEM, VMEM],
        out_specs=VMEM,
        scratch_shapes=[pltpu.VMEM((rows * SUB, LANES), jnp.float32)],
        compiler_params=PARAMS,
        cost_estimate=pl.CostEstimate(
            flops=150 * rows * channels * NS,
            bytes_accessed=14 * rows * channels,
            transcendentals=rows * channels * NS,
        ),
    )(*ends, y, d, rate2, bc, x, gate, skip)


def joined(later, earlier, rate2):
    cut = NS * SUB
    through = jnp.tile(later[cut:], (NS, 1))
    state = jnp.exp2(through * rate2) * earlier[:cut] + later[:cut]
    return jnp.concatenate([state, later[cut:] + earlier[cut:]], axis=0)


def earlier_ends(end, rate2):
    peers = lax.axis_size("ctx")
    if peers <= RADIX:
        return [shifted(end, "ctx", d) for d in range(peers - 1, 0, -1)]
    whole, span = end, 1
    while span < peers:
        away = [d * span for d in range(1, RADIX) if d * span < peers]
        parts = [shifted(whole, "ctx", d) for d in away]
        for part in parts:
            whole = joined(whole, part, rate2)
        span *= RADIX
    return [shifted(whole, "ctx", 1)]


def shards(query, key, value, xin, gate_z, w_bc, dt_low, dt_proj, dt_bias, a_rate, skip):
    rows, channels = xin.shape
    group = query.shape[1] // HD
    assert group * rows == WINDOW and lax.axis_size("ctx") % group == 0
    assert channels == SUB * LANES
    packed = pack(query, key, value, group)
    partial_bc = jnp.dot(xin, w_bc, preferred_element_type=jnp.float32)
    tp = lax.axis_size("tp")
    others = [rotated(partial_bc, "tp", tp, d) for d in range(1, tp)]
    moved = [packed[0]] + [rotated(packed[d], "ctx", group, d) for d in range(1, group)]
    delta = jax.nn.softplus(
        jnp.dot(dt_low, dt_proj, preferred_element_type=jnp.float32) + dt_bias[None, :]
    )
    rate2 = (a_rate * -LOG2E).reshape(NS * SUB, LANES)
    bc = sum(others, partial_bc)
    y, d, end = scan_block(delta, xin, rate2, bc)
    ends = earlier_ends(end, rate2)
    old = None
    if lax.axis_size("ctx") > group:
        old = [shifted(block[1:], "ctx", group) for block in moved]
    outs = attention(moved, old, group)
    back = [outs[0]] + [rotated(outs[d], "ctx", group, d) for d in range(1, group)]
    mixed = finish(ends, y, d, rate2, bc, xin, gate_z, skip[None, :])
    return unpack(back, group), mixed


def solution(mesh):
    two = P("ctx", "tp")
    in_specs = (
        two,
        two,
        two,
        two,
        two,
        P("tp", None),
        P("ctx", None),
        P(None, "tp"),
        P("tp"),
        P(None, "tp"),
        P("tp"),
    )
    return jax.shard_map(
        shards, mesh=mesh, in_specs=in_specs, out_specs=(two, two), check_vma=False
    )
```

time: 314 us -> 98.4 us (0.31)
  the two profiles are of different devices: /device:TPU:18 before, /device:TPU:0 now
where the time goes in v1:
time: 98.4 us; the launch traced here: 98 us
  starting transfers between devices  65.1 us (66%)
  Pallas kernels  22.8 us (23%)
  local copies, waits for them, and re-layouts  3.42 us (3%)
  matrix products  3.13 us (3%)
  waiting for transfers between devices  1.59 us (2%)
  other arithmetic  0.99 us (1%)
    ppermute x17, starting transfers between devices, rotated(): return lax.ppermute(block, axis, route)  41.7 us
    ppermute x7, starting transfers between devices, shifted(): lax.ppermute(block, axis, [(i, i + distance) for i in range(peers - dista...  23.4 us
    pallas_call x1, Pallas kernels, scan_block(): pl.pallas_call(scan_kernel, out_shape=[tiles, tiles, jax.ShapeDtypeStruct...  8.67 us
    pallas_call x1, Pallas kernels, finish(): pl.pallas_call(functools.partial(finish_kernel, len(ends)), out_shape=jax...  8.16 us
    pallas_call x1, Pallas kernels, attention(): pl.pallas_call(functools.partial(attention_kernel, group, rows, with_prev...  4.63 us
    unnamed x22, local copies, waits for them, and re-layouts  3.4 us
  transfers between devices with their start and end apart: 24, of which 1 were waited for; matrix products, arithmetic and copies ran while one was open for 3% of the time, Pallas kernels for 22%

profile of v1, /device:TPU:0, one launch (start us, length us, event | category | flops | bytes accessed | tf_op | source)
XLA Modules:
  0.0 98.0 jit_solution(4450648453432860487)
XLA Ops:
  0.7 1.4 %fusion = f32[256,32]{1,0:T(8,128)S(1)} fusion(bf16[256,1024]{1,0:T(8,128)(2,1)} %refs_11_.1, bf16[1024,32]{0,1:T(8,128)(2,1)} %param.16), kind=kOutput, calls=%fused_computation.4 | convolution fusion | flops 16777216 | bytes 622592 | tf_op jit(solution)/shard_map/dot_general | solution.py:279
  2.1 3.0 %collective-permute-start.15 = (f32[256,32]{1,0:T(8,128)S(1)}, f32[256,32]{1,0:T(8,128)S(1)}, u32[]{:S(2)}, u32[]{:S(2)}) collective-permute-start(f32[256,32]{1,0:T(8,128)S(1)} %fusion), channel_id=1, source_target_pairs={{0,2},{1,3},{2,0},{3,1},{4,6},{5,7},{6,4},{7,5},{8,10},{9,11},{10,... | collective-permute-start | bytes 98312 | tf_op jit(solution)/shard_map/ppermute | solution.py:31
  5.1 1.7 %collective-permute-start.16 = (f32[256,32]{1,0:T(8,128)S(1)}, f32[256,32]{1,0:T(8,128)}, u32[]{:S(2)}, u32[]{:S(2)}) collective-permute-start(f32[256,32]{1,0:T(8,128)S(1)} %fusion), channel_id=1, source_target_pairs={{0,3},{1,0},{2,1},{3,2},{4,7},{5,4},{6,5},{7,6},{8,11},{9,8},{10,9... | collective-permute-start | bytes 98312 | tf_op jit(solution)/shard_map/ppermute | solution.py:31
  9.3 1.6 %collective-permute-start = (bf16[3,256,128]{2,1,0:T(8,128)(2,1)S(1)}, bf16[3,256,128]{2,1,0:T(8,128)(2,1)S(1)}, u32[]{:S(2)}, u32[]{:S(2)}) collective-permute-start(bf16[3,256,128]{2,1,0:T(8,128)(2,1)S(1)} %get-tuple-element.22), channel_id=1, source_target_pairs={{0,4},{4,8},{8,12},{12,16},{16,20},{20,24},{24,28},{28,0},{1,5},{5... | collective-permute-start | bytes 589832 | tf_op jit(solution)/shard_map/ppermute | solution.py:31
  10.9 1.6 %collective-permute-start.1 = (bf16[3,256,128]{2,1,0:T(8,128)(2,1)S(1)}, bf16[3,256,128]{2,1,0:T(8,128)(2,1)S(1)}, u32[]{:S(2)}, u32[]{:S(2)}) collective-permute-start(bf16[3,256,128]{2,1,0:T(8,128)(2,1)S(1)} %get-tuple-element.23), channel_id=1, source_target_pairs={{0,8},{4,12},{8,16},{12,20},{16,24},{20,28},{24,0},{28,4},{1,9},{5... | collective-permute-start | bytes 589832 | tf_op jit(solution)/shard_map/ppermute | solution.py:31
  12.5 1.7 %compare_select_fusion.delta_ref = f32[256,1024]{1,0:T(8,128)} fusion(bf16[256,256]{1,0:T(8,128)(2,1)S(1)} %copy-done.9, bf16[256,1024]{1,0:T(8,128)(2,1)S(1)} %copy-done, f32[1024]{0:T(1024)S(1)} %copy-done.10), kind=kOutput, calls=%fused_computation | convolution fusion | flops 136052736 | bytes 1708032 | tf_op jit(solution)/shard_map/dot_general | solution.py:284
  15.3 1.2 %copy-done.7 = f32[256,1024]{1,0:T(8,128)S(1)} copy-done((f32[256,1024]{1,0:T(8,128)S(1)}, f32[256,1024]{1,0:T(8,128)}, u32[]{:S(2)}) %copy-start.7) | copy-done | bytes 1048600
  16.6 8.7 %shard_map.125 = (f32[2048,128]{1,0:T(8,128)S(1)}, f32[2048,128]{1,0:T(8,128)S(1)}, f32[136,128]{1,0:T(8,128)S(1)}) custom-call(f32[256,1024]{1,0:T(8,128)S(1)} %copy-done.7, bf16[256,1024]{1,0:T(8,128)(2,1)S(1)} %copy-done.4, f32[128,128]{1,0:T(8,128)S(1)} %reshape.8.a_ref.refs_9_, f32[256,32]{1,0:T(8,128)S(1)} %add_add_fusion.bc_ref.refs_10_), custom_call_target="tpu_custom_call" | custom-call | flops 838860800 | bytes 3670016 | tf_op jit(solution)/shard_map/pallas_call | solution.py:185
  25.2 3.4 %collective-permute-start.23 = (f32[136,128]{1,0:T(8,128)S(1)}, f32[136,128]{1,0:T(8,128)S(1)}, u32[]{:S(2)}, u32[]{:S(2)}) collective-permute-start(f32[136,128]{1,0:T(8,128)S(1)} %get-tuple-element.37), channel_id=1, source_target_pairs={{0,4},{4,8},{8,12},{12,16},{16,20},{20,24},{24,28},{1,5},{5,9},{9,... | collective-permute-start | bytes 208904 | tf_op jit(solution)/shard_map/ppermute | solution.py:25
  28.7 3.5 %collective-permute-start.22 = (f32[136,128]{1,0:T(8,128)S(1)}, f32[136,128]{1,0:T(8,128)S(1)}, u32[]{:S(2)}, u32[]{:S(2)}) collective-permute-start(f32[136,128]{1,0:T(8,128)S(1)} %get-tuple-element.37), channel_id=1, source_target_pairs={{0,8},{4,12},{8,16},{12,20},{16,24},{20,28},{1,9},{5,13},{9,17},{1... | collective-permute-start | bytes 208904 | tf_op jit(solution)/shard_map/ppermute | solution.py:25
  32.2 1.2 %collective-permute-start.2 = (bf16[3,256,128]{2,1,0:T(8,128)(2,1)S(1)}, bf16[3,256,128]{2,1,0:T(8,128)(2,1)S(1)}, u32[]{:S(2)}, u32[]{:S(2)}) collective-permute-start(bf16[3,256,128]{2,1,0:T(8,128)(2,1)S(1)} %get-tuple-element.24), channel_id=1, source_target_pairs={{0,12},{4,16},{8,20},{12,24},{16,28},{20,0},{24,4},{28,8},{1,13},{... | collective-permute-start | bytes 589832 | tf_op jit(solution)/shard_map/ppermute | solution.py:31
  33.4 2.2 %collective-permute-start.3 = (bf16[3,256,128]{2,1,0:T(8,128)(2,1)S(1)}, bf16[3,256,128]{2,1,0:T(8,128)(2,1)S(1)}, u32[]{:S(2)}, u32[]{:S(2)}) collective-permute-start(bf16[3,256,128]{2,1,0:T(8,128)(2,1)S(1)} %get-tuple-element.25), channel_id=1, source_target_pairs={{0,16},{4,20},{8,24},{12,28},{16,0},{20,4},{24,8},{28,12},{1,17},{... | collective-permute-start | bytes 589832 | tf_op jit(solution)/shard_map/ppermute | solution.py:31
  35.6 19.5 %collective-permute-start.4 = (bf16[3,256,128]{2,1,0:T(8,128)(2,1)S(1)}, bf16[3,256,128]{2,1,0:T(8,128)(2,1)S(1)}, u32[]{:S(2)}, u32[]{:S(2)}) collective-permute-start(bf16[3,256,128]{2,1,0:T(8,128)(2,1)S(1)} %get-tuple-element.26), channel_id=1, source_target_pairs={{0,20},{4,24},{8,28},{12,0},{16,4},{20,8},{24,12},{28,16},{1,21},{... | collective-permute-start | bytes 589832 | tf_op jit(solution)/shard_map/ppermute | solution.py:31
  56.5 3.9 %collective-permute-start.21 = (f32[136,128]{1,0:T(8,128)S(1)}, f32[136,128]{1,0:T(8,128)S(1)}, u32[]{:S(2)}, u32[]{:S(2)}) collective-permute-start(f32[136,128]{1,0:T(8,128)S(1)} %get-tuple-element.37), channel_id=1, source_target_pairs={{0,12},{4,16},{8,20},{12,24},{16,28},{1,13},{5,17},{9,21},{13,25},... | collective-permute-start | bytes 208904 | tf_op jit(solution)/shard_map/ppermute | solution.py:25
  60.5 1.3 %collective-permute-start.20 = (f32[136,128]{1,0:T(8,128)S(1)}, f32[136,128]{1,0:T(8,128)S(1)}, u32[]{:S(2)}, u32[]{:S(2)}) collective-permute-start(f32[136,128]{1,0:T(8,128)S(1)} %get-tuple-element.37), channel_id=1, source_target_pairs={{0,16},{4,20},{8,24},{12,28},{1,17},{5,21},{9,25},{13,29},{2,18},{... | collective-permute-start | bytes 208904 | tf_op jit(solution)/shard_map/ppermute | solution.py:25
  61.8 6.1 %collective-permute-start.19 = (f32[136,128]{1,0:T(8,128)S(1)}, f32[136,128]{1,0:T(8,128)S(1)}, u32[]{:S(2)}, u32[]{:S(2)}) collective-permute-start(f32[136,128]{1,0:T(8,128)S(1)} %get-tuple-element.37), channel_id=1, source_target_pairs={{0,20},{4,24},{8,28},{1,21},{5,25},{9,29},{2,22},{6,26},{10,30},{3... | collective-permute-start | bytes 208904 | tf_op jit(solution)/shard_map/ppermute | solution.py:25
  67.9 1.5 %collective-permute-start.18 = (f32[136,128]{1,0:T(8,128)S(1)}, f32[136,128]{1,0:T(8,128)S(1)}, u32[]{:S(2)}, u32[]{:S(2)}) collective-permute-start(f32[136,128]{1,0:T(8,128)S(1)} %get-tuple-element.37), channel_id=1, source_target_pairs={{0,24},{4,28},{1,25},{5,29},{2,26},{6,30},{3,27},{7,31}} | collective-permute-start | bytes 208904 | tf_op jit(solution)/shard_map/ppermute | solution.py:25
  69.5 3.6 %collective-permute-start.17 = (f32[136,128]{1,0:T(8,128)S(1)}, f32[136,128]{1,0:T(8,128)S(1)}, u32[]{:S(2)}, u32[]{:S(2)}) collective-permute-start(f32[136,128]{1,0:T(8,128)S(1)} %get-tuple-element.37), channel_id=1, source_target_pairs={{0,28},{1,29},{2,30},{3,31}} | collective-permute-start | bytes 208904 | tf_op jit(solution)/shard_map/ppermute | solution.py:25
  73.1 4.6 %shard_map.123 = (bf16[256,128]{1,0:T(8,128)(2,1)S(1)}, bf16[256,128]{1,0:T(8,128)(2,1)S(1)}, bf16[256,128]{1,0:T(8,128)(2,1)S(1)}, bf16[256,128]{1,0:T(8,128)(2...) custom-call(bf16[3,256,128]{2,1,0:T(8,128)(2,1)S(1)} %get-tuple-elem, ...), custom_call_target="tpu_custom_call" | custom-call | flops 1073741824 | bytes 2097152 | tf_op jit(solution)/shard_map/pallas_call | solution.py:129
  78.0 5.2 %collective-permute-start.10 = (bf16[256,128]{1,0:T(8,128)(2,1)S(1)}, bf16[256,128]{1,0:T(8,128)(2,1)S(1)}, u32[]{:S(2)}, u32[]{:S(2)}) collective-permute-start(bf16[256,128]{1,0:T(8,128)(2,1)S(1)} %get-tuple-element.33), channel_id=1, source_target_pairs={{0,16},{4,20},{8,24},{12,28},{16,0},{20,4},{24,8},{28,12},{1,17},{... | collective-permute-start | bytes 196616 | tf_op jit(solution)/shard_map/ppermute | solution.py:31
  83.3 1.5 %collective-permute-done.7.refs_1_ = bf16[256,128]{1,0:T(8,128)(2,1)S(1)} collective-permute-done((bf16[256,128]{1,0:T(8,128)(2,1)S(1)}, bf16[256,128]{1,0:T(8,128)(2,1)S(1)}, u32[]{:S(2)}, u32[]{:S(2)}) %collective-permute-start.7) | collective-permute-done | bytes 65568 | tf_op jit(solution)/shard_map/ppermute | solution.py:31
  84.8 1.3 %collective-permute-start.12 = (bf16[256,128]{1,0:T(8,128)(2,1)S(1)}, bf16[256,128]{1,0:T(8,128)(2,1)S(1)}, u32[]{:S(2)}, u32[]{:S(2)}) collective-permute-start(bf16[256,128]{1,0:T(8,128)(2,1)S(1)} %get-tuple-element.35), channel_id=1, source_target_pairs={{0,24},{4,28},{8,0},{12,4},{16,8},{20,12},{24,16},{28,20},{1,25},{... | collective-permute-start | bytes 196616 | tf_op jit(solution)/shard_map/ppermute | solution.py:31
  86.1 2.7 %collective-permute-start.13 = (bf16[256,128]{1,0:T(8,128)(2,1)S(1)}, bf16[256,128]{1,0:T(8,128)(2,1)S(1)}, u32[]{:S(2)}, u32[]{:S(2)}) collective-permute-start(bf16[256,128]{1,0:T(8,128)(2,1)S(1)} %get-tuple-element.36), channel_id=1, source_target_pairs={{0,28},{4,0},{8,4},{12,8},{16,12},{20,16},{24,20},{28,24},{1,29},{... | collective-permute-start | bytes 196616 | tf_op jit(solution)/shard_map/ppermute | solution.py:31
  88.8 8.2 %shard_map.126 = bf16[256,1024]{1,0:T(8,128)(2,1)} custom-call(f32[136,128]{1,0:T(8,128)S(1)} %collective-permute-done.17.refs_0_, f32[136,128]{1,0:T(8,128)S(1)} %collective-permute-done.18.refs_1_, f32[136,128]{1,0:T(8,128)S(1)} %collective-permute-done.19.refs_2_, f32[136,128]{1,0:T(8,128)S(1)} %collective-permute-done.20.refs_3_, ...), custom_call_target="tpu_custom_call" | custom-call | flops 629145600 | bytes 3670016 | tf_op jit(solution)/shard_map/pallas_call | solution.py:237
  (56 shorter events, 6.3 us)
Async XLA Ops:
  2.1 12.2 %collective-permute-start.15 = (f32[256,32]{1,0:T(8,128)S(1)}, f32[256,32]{1,0:T(8,128)S(1)}, u32[]{:S(2)}, u32[]{:S(2)}) collective-permute-start(f32[256,32]{1,0:T(8,128)S(1)} %fusion), channel_id=1, source_target_pairs={{0,2},{1,3},{2,0},{3,1},{4,6},{5,7},{6,4},{7,5},{8,10},{9,11},{10,... | collective-permute-start | bytes 98312 | tf_op jit(solution)/shard_map/ppermute | solution.py:31
  5.1 9.2 %collective-permute-start.14 = (f32[256,32]{1,0:T(8,128)S(1)}, f32[256,32]{1,0:T(8,128)S(1)}, u32[]{:S(2)}, u32[]{:S(2)}) collective-permute-start(f32[256,32]{1,0:T(8,128)S(1)} %fusion), channel_id=1, source_target_pairs={{0,1},{1,2},{2,3},{3,0},{4,5},{5,6},{6,7},{7,4},{8,9},{9,10},{10,1... | collective-permute-start | bytes 98312 | tf_op jit(solution)/shard_map/ppermute | solution.py:31
  5.1 9.2 %collective-permute-start.16 = (f32[256,32]{1,0:T(8,128)S(1)}, f32[256,32]{1,0:T(8,128)}, u32[]{:S(2)}, u32[]{:S(2)}) collective-permute-start(f32[256,32]{1,0:T(8,128)S(1)} %fusion), channel_id=1, source_target_pairs={{0,3},{1,0},{2,1},{3,2},{4,7},{5,4},{6,5},{7,6},{8,11},{9,8},{10,9... | collective-permute-start | bytes 98312 | tf_op jit(solution)/shard_map/ppermute | solution.py:31
  9.3 45.7 %collective-permute-start = (bf16[3,256,128]{2,1,0:T(8,128)(2,1)S(1)}, bf16[3,256,128]{2,1,0:T(8,128)(2,1)S(1)}, u32[]{:S(2)}, u32[]{:S(2)}) collective-permute-start(bf16[3,256,128]{2,1,0:T(8,128)(2,1)S(1)} %get-tuple-element.22), channel_id=1, source_target_pairs={{0,4},{4,8},{8,12},{12,16},{16,20},{20,24},{24,28},{28,0},{1,5},{5... | collective-permute-start | bytes 589832 | tf_op jit(solution)/shard_map/ppermute | solution.py:31
  10.9 44.6 %collective-permute-start.1 = (bf16[3,256,128]{2,1,0:T(8,128)(2,1)S(1)}, bf16[3,256,128]{2,1,0:T(8,128)(2,1)S(1)}, u32[]{:S(2)}, u32[]{:S(2)}) collective-permute-start(bf16[3,256,128]{2,1,0:T(8,128)(2,1)S(1)} %get-tuple-element.23), channel_id=1, source_target_pairs={{0,8},{4,12},{8,16},{12,20},{16,24},{20,28},{24,0},{28,4},{1,9},{5... | collective-permute-start | bytes 589832 | tf_op jit(solution)/shard_map/ppermute | solution.py:31
  25.2 8.2 %collective-permute-start.23 = (f32[136,128]{1,0:T(8,128)S(1)}, f32[136,128]{1,0:T(8,128)S(1)}, u32[]{:S(2)}, u32[]{:S(2)}) collective-permute-start(f32[136,128]{1,0:T(8,128)S(1)} %get-tuple-element.37), channel_id=1, source_target_pairs={{0,4},{4,8},{8,12},{12,16},{16,20},{20,24},{24,28},{1,5},{5,9},{9,... | collective-permute-start | bytes 208904 | tf_op jit(solution)/shard_map/ppermute | solution.py:25
  28.7 6.9 %collective-permute-start.22 = (f32[136,128]{1,0:T(8,128)S(1)}, f32[136,128]{1,0:T(8,128)S(1)}, u32[]{:S(2)}, u32[]{:S(2)}) collective-permute-start(f32[136,128]{1,0:T(8,128)S(1)} %get-tuple-element.37), channel_id=1, source_target_pairs={{0,8},{4,12},{8,16},{12,20},{16,24},{20,28},{1,9},{5,13},{9,17},{1... | collective-permute-start | bytes 208904 | tf_op jit(solution)/shard_map/ppermute | solution.py:25
  32.2 24.4 %collective-permute-start.2 = (bf16[3,256,128]{2,1,0:T(8,128)(2,1)S(1)}, bf16[3,256,128]{2,1,0:T(8,128)(2,1)S(1)}, u32[]{:S(2)}, u32[]{:S(2)}) collective-permute-start(bf16[3,256,128]{2,1,0:T(8,128)(2,1)S(1)} %get-tuple-element.24), channel_id=1, source_target_pairs={{0,12},{4,16},{8,20},{12,24},{16,28},{20,0},{24,4},{28,8},{1,13},{... | collective-permute-start | bytes 589832 | tf_op jit(solution)/shard_map/ppermute | solution.py:31
  33.4 27.1 %collective-permute-start.3 = (bf16[3,256,128]{2,1,0:T(8,128)(2,1)S(1)}, bf16[3,256,128]{2,1,0:T(8,128)(2,1)S(1)}, u32[]{:S(2)}, u32[]{:S(2)}) collective-permute-start(bf16[3,256,128]{2,1,0:T(8,128)(2,1)S(1)} %get-tuple-element.25), channel_id=1, source_target_pairs={{0,16},{4,20},{8,24},{12,28},{16,0},{20,4},{24,8},{28,12},{1,17},{... | collective-permute-start | bytes 589832 | tf_op jit(solution)/shard_map/ppermute | solution.py:31
  35.6 26.2 %collective-permute-start.4 = (bf16[3,256,128]{2,1,0:T(8,128)(2,1)S(1)}, bf16[3,256,128]{2,1,0:T(8,128)(2,1)S(1)}, u32[]{:S(2)}, u32[]{:S(2)}) collective-permute-start(bf16[3,256,128]{2,1,0:T(8,128)(2,1)S(1)} %get-tuple-element.26), channel_id=1, source_target_pairs={{0,20},{4,24},{8,28},{12,0},{16,4},{20,8},{24,12},{28,16},{1,21},{... | collective-permute-start | bytes 589832 | tf_op jit(solution)/shard_map/ppermute | solution.py:31
  55.1 12.9 %collective-permute-start.5 = (bf16[3,256,128]{2,1,0:T(8,128)(2,1)S(1)}, bf16[3,256,128]{2,1,0:T(8,128)(2,1)S(1)}, u32[]{:S(2)}, u32[]{:S(2)}) collective-permute-start(bf16[3,256,128]{2,1,0:T(8,128)(2,1)S(1)} %get-tuple-element.27), channel_id=1, source_target_pairs={{0,24},{4,28},{8,0},{12,4},{16,8},{20,12},{24,16},{28,20},{1,25},{... | collective-permute-start | bytes 589832 | tf_op jit(solution)/shard_map/ppermute | solution.py:31
  55.5 13.9 %collective-permute-start.6 = (bf16[3,256,128]{2,1,0:T(8,128)(2,1)S(1)}, bf16[3,256,128]{2,1,0:T(8,128)(2,1)S(1)}, u32[]{:S(2)}, u32[]{:S(2)}) collective-permute-start(bf16[3,256,128]{2,1,0:T(8,128)(2,1)S(1)} %get-tuple-element.28), channel_id=1, source_target_pairs={{0,28},{4,0},{8,4},{12,8},{16,12},{20,16},{24,20},{28,24},{1,29},{... | collective-permute-start | bytes 589832 | tf_op jit(solution)/shard_map/ppermute | solution.py:31
  56.5 21.2 %collective-permute-start.21 = (f32[136,128]{1,0:T(8,128)S(1)}, f32[136,128]{1,0:T(8,128)S(1)}, u32[]{:S(2)}, u32[]{:S(2)}) collective-permute-start(f32[136,128]{1,0:T(8,128)S(1)} %get-tuple-element.37), channel_id=1, source_target_pairs={{0,12},{4,16},{8,20},{12,24},{16,28},{1,13},{5,17},{9,21},{13,25},... | collective-permute-start | bytes 208904 | tf_op jit(solution)/shard_map/ppermute | solution.py:25
  60.5 17.4 %collective-permute-start.20 = (f32[136,128]{1,0:T(8,128)S(1)}, f32[136,128]{1,0:T(8,128)S(1)}, u32[]{:S(2)}, u32[]{:S(2)}) collective-permute-start(f32[136,128]{1,0:T(8,128)S(1)} %get-tuple-element.37), channel_id=1, source_target_pairs={{0,16},{4,20},{8,24},{12,28},{1,17},{5,21},{9,25},{13,29},{2,18},{... | collective-permute-start | bytes 208904 | tf_op jit(solution)/shard_map/ppermute | solution.py:25
  61.8 16.1 %collective-permute-start.19 = (f32[136,128]{1,0:T(8,128)S(1)}, f32[136,128]{1,0:T(8,128)S(1)}, u32[]{:S(2)}, u32[]{:S(2)}) collective-permute-start(f32[136,128]{1,0:T(8,128)S(1)} %get-tuple-element.37), channel_id=1, source_target_pairs={{0,20},{4,24},{8,28},{1,21},{5,25},{9,29},{2,22},{6,26},{10,30},{3... | collective-permute-start | bytes 208904 | tf_op jit(solution)/shard_map/ppermute | solution.py:25
  67.9 10.1 %collective-permute-start.18 = (f32[136,128]{1,0:T(8,128)S(1)}, f32[136,128]{1,0:T(8,128)S(1)}, u32[]{:S(2)}, u32[]{:S(2)}) collective-permute-start(f32[136,128]{1,0:T(8,128)S(1)} %get-tuple-element.37), channel_id=1, source_target_pairs={{0,24},{4,28},{1,25},{5,29},{2,26},{6,30},{3,27},{7,31}} | collective-permute-start | bytes 208904 | tf_op jit(solution)/shard_map/ppermute | solution.py:25
  69.5 13.7 %collective-permute-start.17 = (f32[136,128]{1,0:T(8,128)S(1)}, f32[136,128]{1,0:T(8,128)S(1)}, u32[]{:S(2)}, u32[]{:S(2)}) collective-permute-start(f32[136,128]{1,0:T(8,128)S(1)} %get-tuple-element.37), channel_id=1, source_target_pairs={{0,28},{1,29},{2,30},{3,31}} | collective-permute-start | bytes 208904 | tf_op jit(solution)/shard_map/ppermute | solution.py:25
  77.8 7.0 %collective-permute-start.7 = (bf16[256,128]{1,0:T(8,128)(2,1)S(1)}, bf16[256,128]{1,0:T(8,128)(2,1)S(1)}, u32[]{:S(2)}, u32[]{:S(2)}) collective-permute-start(bf16[256,128]{1,0:T(8,128)(2,1)S(1)} %get-tuple-element.30), channel_id=1, source_target_pairs={{0,4},{4,8},{8,12},{12,16},{16,20},{20,24},{24,28},{28,0},{1,5},{5... | collective-permute-start | bytes 196616 | tf_op jit(solution)/shard_map/ppermute | solution.py:31
  77.9 8.3 %collective-permute-start.8 = (bf16[256,128]{1,0:T(8,128)(2,1)S(1)}, bf16[256,128]{1,0:T(8,128)(2,1)S(1)}, u32[]{:S(2)}, u32[]{:S(2)}) collective-permute-start(bf16[256,128]{1,0:T(8,128)(2,1)S(1)} %get-tuple-element.31), channel_id=1, source_target_pairs={{0,8},{4,12},{8,16},{12,20},{16,24},{20,28},{24,0},{28,4},{1,9},{5... | collective-permute-start | bytes 196616 | tf_op jit(solution)/shard_map/ppermute | solution.py:31
  77.9 19.1 %collective-permute-start.9 = (bf16[256,128]{1,0:T(8,128)(2,1)S(1)}, bf16[256,128]{1,0:T(8,128)(2,1)S(1)}, u32[]{:S(2)}, u32[]{:S(2)}) collective-permute-start(bf16[256,128]{1,0:T(8,128)(2,1)S(1)} %get-tuple-element.32), channel_id=1, source_target_pairs={{0,12},{4,16},{8,20},{12,24},{16,28},{20,0},{24,4},{28,8},{1,13},{... | collective-permute-start | bytes 196616 | tf_op jit(solution)/shard_map/ppermute | solution.py:31
  78.0 19.0 %collective-permute-start.10 = (bf16[256,128]{1,0:T(8,128)(2,1)S(1)}, bf16[256,128]{1,0:T(8,128)(2,1)S(1)}, u32[]{:S(2)}, u32[]{:S(2)}) collective-permute-start(bf16[256,128]{1,0:T(8,128)(2,1)S(1)} %get-tuple-element.33), channel_id=1, source_target_pairs={{0,16},{4,20},{8,24},{12,28},{16,0},{20,4},{24,8},{28,12},{1,17},{... | collective-permute-start | bytes 196616 | tf_op jit(solution)/shard_map/ppermute | solution.py:31
  83.2 13.8 %collective-permute-start.11 = (bf16[256,128]{1,0:T(8,128)(2,1)S(1)}, bf16[256,128]{1,0:T(8,128)(2,1)S(1)}, u32[]{:S(2)}, u32[]{:S(2)}) collective-permute-start(bf16[256,128]{1,0:T(8,128)(2,1)S(1)} %get-tuple-element.34), channel_id=1, source_target_pairs={{0,20},{4,24},{8,28},{12,0},{16,4},{20,8},{24,12},{28,16},{1,21},{... | collective-permute-start | bytes 196616 | tf_op jit(solution)/shard_map/ppermute | solution.py:31
  84.8 12.2 %collective-permute-start.12 = (bf16[256,128]{1,0:T(8,128)(2,1)S(1)}, bf16[256,128]{1,0:T(8,128)(2,1)S(1)}, u32[]{:S(2)}, u32[]{:S(2)}) collective-permute-start(bf16[256,128]{1,0:T(8,128)(2,1)S(1)} %get-tuple-element.35), channel_id=1, source_target_pairs={{0,24},{4,28},{8,0},{12,4},{16,8},{20,12},{24,16},{28,20},{1,25},{... | collective-permute-start | bytes 196616 | tf_op jit(solution)/shard_map/ppermute | solution.py:31
  86.1 10.9 %collective-permute-start.13 = (bf16[256,128]{1,0:T(8,128)(2,1)S(1)}, bf16[256,128]{1,0:T(8,128)(2,1)S(1)}, u32[]{:S(2)}, u32[]{:S(2)}) collective-permute-start(bf16[256,128]{1,0:T(8,128)(2,1)S(1)} %get-tuple-element.36), channel_id=1, source_target_pairs={{0,28},{4,0},{8,4},{12,8},{16,12},{20,16},{24,20},{28,24},{1,29},{... | collective-permute-start | bytes 196616 | tf_op jit(solution)/shard_map/ppermute | solution.py:31
  (11 other events, 69.2 us)

commit v2 on v1

--- a/solution.py
+++ b/solution.py
@@ -258,8 +258,6 @@
 
 def earlier_ends(end, rate2):
     peers = lax.axis_size("ctx")
-    if peers <= RADIX:
-        return [shifted(end, "ctx", d) for d in range(peers - 1, 0, -1)]
     whole, span = end, 1
     while span < peers:
         away = [d * span for d in range(1, RADIX) if d * span < peers]
@@ -270,26 +268,234 @@
     return [shifted(whole, "ctx", 1)]
 
 
+def send(src, dst, sems, at, axis, peer):
+    return pltpu.make_async_remote_copy(
+        src_ref=src,
+        dst_ref=dst,
+        send_sem=sems.at[0, at],
+        recv_sem=sems.at[1, at],
+        device_id={axis: peer},
+        device_id_type=pl.DeviceIdType.MESH,
+    )
+
+
+def whole_kernel(group, tp, *refs):
+    q_ref, k_ref, v_ref, x_ref, gate_ref, delta_ref, part_ref, a_ref, skip_ref = refs[:9]
+    att_ref, mix_ref = refs[9:11]
+    (pack_s, got_s, bcs_s, bc_v, bc_s, y_s, d_s, u_s, end_s, ends_s, inc_s, o_s, back_s) = refs[11:24]
+    bc_sem, qkv_sem, end_sem, out_sem, copy_sem = refs[24:]
+    rows = x_ref.shape[0]
+    slot = lax.axis_index("ctx")
+    line = lax.axis_index("tp")
+    peer = [lax.rem(slot + d, group) for d in range(group)]
+    origin = [lax.rem(slot - d + group, group) for d in range(group)]
+
+    barrier = pltpu.get_barrier_semaphore()
+    for d in range(1, group):
+        pl.semaphore_signal(
+            barrier, inc=1, device_id={"ctx": peer[d]}, device_id_type=pl.DeviceIdType.MESH
+        )
+    for d in range(1, tp):
+        pl.semaphore_signal(
+            barrier,
+            inc=1,
+            device_id={"tp": lax.rem(line + d, tp)},
+            device_id_type=pl.DeviceIdType.MESH,
+        )
+    for d in range(1, group):
+        col = pl.ds(pl.multiple_of(peer[d] * HD, HD), HD)
+        for part, ref in enumerate((q_ref, k_ref, v_ref)):
+            pack_s[d - 1, part] = ref[:, col]
+    col = pl.ds(pl.multiple_of(slot * HD, HD), HD)
+    for part, ref in enumerate((q_ref, k_ref, v_ref)):
+        got_s[slot, part] = ref[:, col]
+    pl.semaphore_wait(barrier, group + tp - 2)
+
+    bc_copies = [
+        send(part_ref, bcs_s.at[d - 1], bc_sem, d - 1, "tp", lax.rem(line + d, tp))
+        for d in range(1, tp)
+    ]
+    for copy in bc_copies:
+        copy.start()
+    qkv_copies = [
+        send(pack_s.at[d - 1], got_s.at[slot], qkv_sem, d - 1, "ctx", peer[d])
+        for d in range(1, group)
+    ]
+    for copy in qkv_copies:
+        copy.start()
+
+    for c in range(SUB):
+        cols = slice(c * LANES, (c + 1) * LANES)
+        dt = delta_ref[:, cols]
+        d_s[pl.ds(c, rows, stride=SUB), :] = dt
+        u_s[pl.ds(c, rows, stride=SUB), :] = dt * x_ref[:, cols].astype(jnp.float32)
+    total = part_ref[...]
+    for d in range(1, tp):
+        bc_copies[d - 1].wait()
+        total = total + bcs_s[d - 1]
+    bc_v[...] = total
+    to_scalars = pltpu.make_async_copy(bc_v, bc_s, copy_sem)
+    to_scalars.start()
+    to_scalars.wait()
+
+    tile = [slice(n * SUB, (n + 1) * SUB) for n in range(NS + 1)]
+    per = 4
+
+    def step(block, carry):
+        states, through = list(carry[:NS]), carry[NS]
+        for k in range(per):
+            t = block * per + k
+            at = pl.ds(pl.multiple_of(t * SUB, SUB), SUB)
+            dt, u = d_s[at, :], u_s[at, :]
+            through = through + dt
+            sums = [None] * 4
+            for n in range(NS):
+                e = jnp.exp2(dt * a_ref[tile[n], :])
+                states[n] = e * states[n] + u * bc_s[n, t]
+                term = states[n] * bc_s[NS + n, t]
+                sums[n % 4] = term if n < 4 else sums[n % 4] + term
+            y_s[at, :] = (sums[0] + sums[1]) + (sums[2] + sums[3])
+        return (*states, through)
+
+    zero = jnp.zeros((SUB, LANES), jnp.float32)
+    ends = lax.fori_loop(0, rows // per, step, (zero,) * (NS + 1))
+    for n in range(NS + 1):
+        end_s[tile[n], :] = ends[n]
+
+    end_copies = [
+        send(end_s, ends_s.at[d - 1], end_sem, d - 1, "ctx", peer[d]) for d in range(1, group)
+    ]
+    for d in range(1, group):
+        pl.when(slot + d < group)(end_copies[d - 1].start)
+
+    for copy in qkv_copies:
+        copy.wait()
+    row = lax.broadcasted_iota(jnp.int32, (rows, rows), 0)
+    col = lax.broadcasted_iota(jnp.int32, (rows, rows), 1)
+    factor = HD**-0.5 * LOG2E
+    for i in range(group):
+        q = got_s[i, 0]
+        keys = got_s[: i + 1, 1].reshape((i + 1) * rows, HD)
+        values = got_s[: i + 1, 2].reshape((i + 1) * rows, HD)
+        s = lax.dot_general(
+            q, keys, (((1,), (1,)), ((), ())), preferred_element_type=jnp.float32
+        )
+        last = jnp.where(col <= row, s[:, i * rows :], -jnp.inf)
+        s = jnp.concatenate([s[:, : i * rows], last], axis=1) if i else last
+        top = jnp.max(s, axis=1, keepdims=True)
+        p = jnp.exp2((s - top) * factor)
+        o = jnp.dot(p.astype(jnp.bfloat16), values, preferred_element_type=jnp.float32)
+        o_s[i] = (o / jnp.sum(p, axis=1, keepdims=True)).astype(jnp.bfloat16)
+
+    out_copies = [
+        send(o_s.at[peer[d]], back_s.at[d - 1], out_sem, d - 1, "ctx", peer[d])
+        for d in range(1, group)
+    ]
+    for copy in out_copies:
+        copy.start()
+
+    inc_s[...] = jnp.zeros_like(inc_s)
+    for d in range(group - 1, 0, -1):
+
+        @pl.when(slot >= d)
+        def _(d=d):
+            end_copies[d - 1].wait_recv()
+            through = ends_s[d - 1, tile[NS], :]
+            for n in range(NS):
+                inc_s[tile[n], :] = (
+                    jnp.exp2(through * a_ref[tile[n], :]) * inc_s[tile[n], :]
+                    + ends_s[d - 1, tile[n], :]
+                )
+
+    def correct(block, carry):
+        held = list(carry)
+        for k in range(per):
+            t = block * per + k
+            at = pl.ds(pl.multiple_of(t * SUB, SUB), SUB)
+            dt = d_s[at, :]
+            sums = [y_s[at, :], None, None, None]
+            for n in range(NS):
+                held[n] = jnp.exp2(dt * a_ref[tile[n], :]) * held[n]
+                term = held[n] * bc_s[NS + n, t]
+                sums[n % 4] = term if sums[n % 4] is None else sums[n % 4] + term
+            y_s[at, :] = (sums[0] + sums[1]) + (sums[2] + sums[3])
+        return tuple(held)
+
+    lax.fori_loop(0, rows // per, correct, tuple(inc_s[tile[n], :] for n in range(NS)))
+    for c in range(SUB):
+        cols = slice(c * LANES, (c + 1) * LANES)
+        y = y_s[pl.ds(c, rows, stride=SUB), :] + skip_ref[:, cols] * x_ref[:, cols].astype(jnp.float32)
+        g = gate_ref[:, cols].astype(jnp.float32)
+        mix_ref[:, cols] = (y * (g / (1.0 + jnp.exp(-g)))).astype(mix_ref.dtype)
+
+    att_ref[:, pl.ds(pl.multiple_of(slot * HD, HD), HD)] = o_s[slot]
+    for d in range(1, group):
+        out_copies[d - 1].wait()
+        att_ref[:, pl.ds(pl.multiple_of(origin[d] * HD, HD), HD)] = back_s[d - 1]
+    for d in range(1, group):
+        pl.when(slot + d < group)(end_copies[d - 1].wait_send)
+
+
+def whole(query, key, value, xin, gate_z, delta, part, rate2, skip):
+    rows, channels = xin.shape
+    group, tp = lax.axis_size("ctx"), lax.axis_size("tp")
+    f32, bf16 = jnp.float32, jnp.bfloat16
+    tiles = pltpu.VMEM((rows * SUB, LANES), f32)
+    ends = ((NS + 1) * SUB, LANES)
+    return pl.pallas_call(
+        functools.partial(whole_kernel, group, tp),
+        out_shape=[jax.ShapeDtypeStruct((rows, channels), bf16)] * 2,
+        in_specs=[VMEM] * 9,
+        out_specs=[VMEM] * 2,
+        scratch_shapes=[
+            pltpu.VMEM((group - 1, 3, rows, HD), bf16),
+            pltpu.VMEM((group, 3, rows, HD), bf16),
+            pltpu.VMEM((tp - 1, 2 * NS, rows), f32),
+            pltpu.VMEM((2 * NS, rows), f32),
+            pltpu.SMEM((2 * NS, rows), f32),
+            tiles,
+            tiles,
+            tiles,
+            pltpu.VMEM(ends, f32),
+            pltpu.VMEM((group - 1, *ends), f32),
+            pltpu.VMEM((NS * SUB, LANES), f32),
+            pltpu.VMEM((group, rows, HD), bf16),
+            pltpu.VMEM((group - 1, rows, HD), bf16),
+            pltpu.SemaphoreType.DMA((2, tp - 1)),
+            pltpu.SemaphoreType.DMA((2, group - 1)),
+            pltpu.SemaphoreType.DMA((2, group - 1)),
+            pltpu.SemaphoreType.DMA((2, group - 1)),
+            pltpu.SemaphoreType.DMA,
+        ],
+        compiler_params=pltpu.CompilerParams(
+            collective_id=0, has_side_effects=True, vmem_limit_bytes=40 * 1024 * 1024
+        ),
+    )(query, key, value, xin, gate_z, delta, part, rate2, skip)
+
+
 def shards(query, key, value, xin, gate_z, w_bc, dt_low, dt_proj, dt_bias, a_rate, skip):
     rows, channels = xin.shape
     group = query.shape[1] // HD
     assert group * rows == WINDOW and lax.axis_size("ctx") % group == 0
     assert channels == SUB * LANES
+    delta = jax.nn.softplus(
+        jnp.dot(dt_low, dt_proj, preferred_element_type=jnp.float32) + dt_bias[None, :]
+    )
+    rate2 = (a_rate * -LOG2E).reshape(NS * SUB, LANES)
+    if lax.axis_size("ctx") == group:
+        part = lax.dot_general(
+            w_bc, xin, (((0,), (1,)), ((), ())), preferred_element_type=jnp.float32
+        )
+        return tuple(whole(query, key, value, xin, gate_z, delta, part, rate2, skip[None, :]))
     packed = pack(query, key, value, group)
     partial_bc = jnp.dot(xin, w_bc, preferred_element_type=jnp.float32)
     tp = lax.axis_size("tp")
     others = [rotated(partial_bc, "tp", tp, d) for d in range(1, tp)]
     moved = [packed[0]] + [rotated(packed[d], "ctx", group, d) for d in range(1, group)]
-    delta = jax.nn.softplus(
-        jnp.dot(dt_low, dt_proj, preferred_element_type=jnp.float32) + dt_bias[None, :]
-    )
-    rate2 = (a_rate * -LOG2E).reshape(NS * SUB, LANES)
     bc = sum(others, partial_bc)
     y, d, end = scan_block(delta, xin, rate2, bc)
     ends = earlier_ends(end, rate2)
-    old = None
-    if lax.axis_size("ctx") > group:
-        old = [shifted(block[1:], "ctx", group) for block in moved]
+    old = [shifted(block[1:], "ctx", group) for block in moved]
     outs = attention(moved, old, group)
     back = [outs[0]] + [rotated(outs[d], "ctx", group, d) for d in range(1, group)]
     mixed = finish(ends, y, d, rate2, bc, xin, gate_z, skip[None, :])

time: 98.4 us -> 71.3 us (0.72)
  starting transfers between devices: 65.1 us -> 0 us
  Pallas kernels: 22.8 us -> 64.8 us
  waiting for transfers between devices: 1.59 us -> 0 us
    ppermute x24 -> x0, starting transfers between devices: 65.1 us -> none  [the longest x17 41.7 us: rotated(): return lax.ppermute(block, axis, route)]
    pallas_call x5 -> x1, Pallas kernels: 22.8 us -> 64.8 us  [whole(): pl.pallas_call(functools.partial(whole_kernel, group, tp), out_shape=[jax...]
    ppermute x24 -> x0, waiting for transfers between devices: 1.59 us -> none  [the longest x17 1.57 us: rotated(): return lax.ppermute(block, axis, route)]
  transfers between devices with their start and end apart: 24 -> 0, of which waited for: 1 -> 0; matrix products, arithmetic and copies ran while one was open for 3% -> 0% of each run, Pallas kernels for 22% -> 0%
where the time goes in v2:
time: 71.3 us; the launch traced here: 71.1 us
  Pallas kernels  64.8 us (91%)
  local copies, waits for them, and re-layouts  3.36 us (5%)
  matrix products  2.15 us (3%)
  between operations  0.76 us (1%)
    pallas_call x1, Pallas kernels, whole(): pl.pallas_call(functools.partial(whole_kernel, group, tp), out_shape=[jax...  64.8 us
    unnamed x22, local copies, waits for them, and re-layouts  3.34 us

profile of v2, /device:TPU:0, one launch (start us, length us, event | category | flops | bytes accessed | tf_op | source)
XLA Modules:
  0.0 71.1 jit_solution(10619411199707208179)
XLA Ops:
  0.6 0.0 copy-start
  0.6 0.0 copy-start.7
  0.7 1.4 %fusion.refs_6_ = f32[32,256]{1,0:T(8,128)S(1)} fusion(bf16[1024,32]{0,1:T(8,128)(2,1)} %param.16, bf16[256,1024]{1,0:T(8,128)(2,1)} %refs_3_.1), kind=kOutput, calls=%fused_computation.3 | convolution fusion | flops 16777216 | bytes 622592 | tf_op jit(solution)/shard_map/dot_general | solution.py:486
  2.1 0.0 copy-done.7
  2.1 0.0 copy-start.8
  2.1 0.0 copy-start.9
  2.1 0.0 copy-done
  2.2 0.8 %copy-done.8 = bf16[256,256]{1,0:T(8,128)(2,1)S(1)} copy-done((bf16[256,256]{1,0:T(8,128)(2,1)S(1)}, bf16[256,256]{1,0:T(8,128)(2,1)}, u32[]{:S(2)}) %copy-start.8) | copy-done | bytes 131096
  3.0 0.0 copy-done.9
  3.0 0.0 copy-start.1
  3.0 0.0 copy-start.2
  3.0 0.0 copy-start.4
  3.0 0.0 copy-start.5
  3.0 0.0 copy-start.6
  3.0 0.7 %compare_select_fusion.refs_5_ = f32[256,1024]{1,0:T(8,128)S(1)} fusion(bf16[256,256]{1,0:T(8,128)(2,1)S(1)} %copy-done.8, bf16[256,1024]{1,0:T(8,128)(2,1)S(1)} %copy-done, f32[1024]{0:T(1024)S(1)} %copy-done.9), kind=kOutput, calls=%fused_computation | convolution fusion | flops 136052736 | bytes 1708032 | tf_op jit(solution)/shard_map/dot_general | solution.py:482
  3.8 0.2 copy-done.1
  4.0 0.2 copy-done.2
  4.2 0.2 copy-done.3
  4.3 0.2 copy-done.4
  4.5 0.2 copy-done.5
  4.7 0.0 copy-done.6
  4.7 64.8 %shard_map.122 = (bf16[256,1024]{1,0:T(8,128)(2,1)S(1)}, bf16[256,1024]{1,0:T(8,128)(2,1)S(1)}) custom-call(bf16[256,1024]{1,0:T(8,128)(2,1)S(1)} %copy-done.2, bf16[256,1024]{1,0:T(8,128)(2,1)S(1)} %copy-done.3, bf16[256,1024]{1,0:T(8,128)(2,1)S(1)} %copy-done.4, bf16[256,1024]{1,0:T(8,128)(2,1)S(1)} %copy-done.1, bf16[256,1024]{1,0:T(8,128)(2,1)S(1)} %copy-done.5, ...), custom_call_target="tpu_custom_call" | custom-call | tf_op jit(solution)/shard_map/pallas_call | solution.py:445
  69.5 0.8 %copy.15 = bf16[256,1024]{1,0:T(8,128)(2,1)} copy(bf16[256,1024]{1,0:T(8,128)(2,1)S(1)} %get-tuple-element.4) | data formatting | bytes 1048576
  70.3 0.8 %copy.16 = bf16[256,1024]{1,0:T(8,128)(2,1)} copy(bf16[256,1024]{1,0:T(8,128)(2,1)S(1)} %get-tuple-element.5) | data formatting | bytes 1048576
  (3 shorter events, 0.0 us)
Async XLA Ops:
  0.6 1.5 %copy-start = (bf16[256,1024]{1,0:T(8,128)(2,1)S(1)}, bf16[256,1024]{1,0:T(8,128)(2,1)}, u32[]{:S(2)}) copy-start(bf16[256,1024]{1,0:T(8,128)(2,1)} %param.18) | copy-start | bytes 1572868
  0.6 1.4 %copy-start.7 = (f32[16,1024]{1,0:T(8,128)S(1)}, f32[16,1024]{1,0:T(8,128)}, u32[]{:S(2)}) copy-start(f32[16,1024]{1,0:T(8,128)} %param.20) | copy-start | bytes 196612
  2.1 0.9 %copy-start.8 = (bf16[256,256]{1,0:T(8,128)(2,1)S(1)}, bf16[256,256]{1,0:T(8,128)(2,1)}, u32[]{:S(2)}) copy-start(bf16[256,256]{1,0:T(8,128)(2,1)} %param.17) | copy-start | bytes 393220
  2.1 0.9 %copy-start.9 = (f32[1024]{0:T(1024)S(1)}, f32[1024]{0:T(1024)}, u32[]{:S(2)}) copy-start(f32[1024]{0:T(1024)} %param.19) | copy-start | bytes 12292
  3.0 1.0 %copy-start.1 = (bf16[256,1024]{1,0:T(8,128)(2,1)S(1)}, bf16[256,1024]{1,0:T(8,128)(2,1)}, u32[]{:S(2)}) copy-start(bf16[256,1024]{1,0:T(8,128)(2,1)} %refs_3_.1) | copy-start | bytes 1572868
  3.0 1.2 %copy-start.2 = (bf16[256,1024]{1,0:T(8,128)(2,1)S(1)}, bf16[256,1024]{1,0:T(8,128)(2,1)}, u32[]{:S(2)}) copy-start(bf16[256,1024]{1,0:T(8,128)(2,1)} %refs_0_.1) | copy-start | bytes 1572868
  3.0 1.4 %copy-start.3 = (bf16[256,1024]{1,0:T(8,128)(2,1)S(1)}, bf16[256,1024]{1,0:T(8,128)(2,1)}, u32[]{:S(2)}) copy-start(bf16[256,1024]{1,0:T(8,128)(2,1)} %refs_1_.1) | copy-start | bytes 1572868
  3.0 1.5 %copy-start.4 = (bf16[256,1024]{1,0:T(8,128)(2,1)S(1)}, bf16[256,1024]{1,0:T(8,128)(2,1)}, u32[]{:S(2)}) copy-start(bf16[256,1024]{1,0:T(8,128)(2,1)} %refs_2_.1) | copy-start | bytes 1572868
  3.0 1.7 %copy-start.5 = (bf16[256,1024]{1,0:T(8,128)(2,1)S(1)}, bf16[256,1024]{1,0:T(8,128)(2,1)}, u32[]{:S(2)}) copy-start(bf16[256,1024]{1,0:T(8,128)(2,1)} %refs_4_.1) | copy-start | bytes 1572868
  3.0 1.6 %copy-start.6 = (f32[1024]{0:T(1024)S(1)}, f32[1024]{0:T(1024)}, u32[]{:S(2)}) copy-start(f32[1024]{0:T(1024)} %param.21) | copy-start | bytes 12292

commit v3 on v2

--- a/solution.py
+++ b/solution.py
@@ -282,13 +282,12 @@
 def whole_kernel(group, tp, *refs):
     q_ref, k_ref, v_ref, x_ref, gate_ref, delta_ref, part_ref, a_ref, skip_ref = refs[:9]
     att_ref, mix_ref = refs[9:11]
-    (pack_s, got_s, bcs_s, bc_v, bc_s, y_s, d_s, u_s, end_s, ends_s, inc_s, o_s, back_s) = refs[11:24]
-    bc_sem, qkv_sem, end_sem, out_sem, copy_sem = refs[24:]
+    (pack_s, got_s, bcs_s, bc_v, bc_s, y_s, d_s, u_s, end_s, ends_s, inc_s, all_s, first_s, o_s, back_s) = refs[11:26]
+    bc_sem, qkv_sem, end_sem, first_sem, out_sem, copy_sem = refs[26:]
     rows = x_ref.shape[0]
     slot = lax.axis_index("ctx")
     line = lax.axis_index("tp")
     peer = [lax.rem(slot + d, group) for d in range(group)]
-    origin = [lax.rem(slot - d + group, group) for d in range(group)]
 
     barrier = pltpu.get_barrier_semaphore()
     for d in range(1, group):
@@ -362,42 +361,20 @@
     for n in range(NS + 1):
         end_s[tile[n], :] = ends[n]
 
+    half = group // 2
+    place = lax.rem(slot, half)
     end_copies = [
-        send(end_s, ends_s.at[d - 1], end_sem, d - 1, "ctx", peer[d]) for d in range(1, group)
+        send(end_s, ends_s.at[d - 1], end_sem, d - 1, "ctx", peer[d]) for d in range(1, half)
     ]
-    for d in range(1, group):
-        pl.when(slot + d < group)(end_copies[d - 1].start)
+    for d in range(1, half):
+        pl.when(place + d < half)(end_copies[d - 1].start)
 
     for copy in qkv_copies:
         copy.wait()
-    row = lax.broadcasted_iota(jnp.int32, (rows, rows), 0)
-    col = lax.broadcasted_iota(jnp.int32, (rows, rows), 1)
-    factor = HD**-0.5 * LOG2E
-    for i in range(group):
-        q = got_s[i, 0]
-        keys = got_s[: i + 1, 1].reshape((i + 1) * rows, HD)
-        values = got_s[: i + 1, 2].reshape((i + 1) * rows, HD)
-        s = lax.dot_general(
-            q, keys, (((1,), (1,)), ((), ())), preferred_element_type=jnp.float32
-        )
-        last = jnp.where(col <= row, s[:, i * rows :], -jnp.inf)
-        s = jnp.concatenate([s[:, : i * rows], last], axis=1) if i else last
-        top = jnp.max(s, axis=1, keepdims=True)
-        p = jnp.exp2((s - top) * factor)
-        o = jnp.dot(p.astype(jnp.bfloat16), values, preferred_element_type=jnp.float32)
-        o_s[i] = (o / jnp.sum(p, axis=1, keepdims=True)).astype(jnp.bfloat16)
-
-    out_copies = [
-        send(o_s.at[peer[d]], back_s.at[d - 1], out_sem, d - 1, "ctx", peer[d])
-        for d in range(1, group)
-    ]
-    for copy in out_copies:
-        copy.start()
-
     inc_s[...] = jnp.zeros_like(inc_s)
-    for d in range(group - 1, 0, -1):
-
-        @pl.when(slot >= d)
+    for d in range(half - 1, 0, -1):
+
+        @pl.when(place >= d)
         def _(d=d):
             end_copies[d - 1].wait_recv()
             through = ends_s[d - 1, tile[NS], :]
@@ -406,6 +383,79 @@
                     jnp.exp2(through * a_ref[tile[n], :]) * inc_s[tile[n], :]
                     + ends_s[d - 1, tile[n], :]
                 )
+            inc_s[tile[NS], :] = inc_s[tile[NS], :] + through
+
+    first_copies = [
+        pltpu.make_async_remote_copy(
+            src_ref=all_s,
+            dst_ref=first_s,
+            send_sem=first_sem.at[1 + k],
+            recv_sem=first_sem.at[0],
+            device_id={"ctx": half + k},
+            device_id_type=pl.DeviceIdType.MESH,
+        )
+        for k in range(group - half)
+    ]
+
+    @pl.when(slot == half - 1)
+    def _():
+        through = end_s[tile[NS], :]
+        for n in range(NS):
+            all_s[tile[n], :] = (
+                jnp.exp2(through * a_ref[tile[n], :]) * inc_s[tile[n], :] + end_s[tile[n], :]
+            )
+        for copy in first_copies:
+            copy.start()
+
+    row = lax.broadcasted_iota(jnp.int32, (rows, rows), 0)
+    col = lax.broadcasted_iota(jnp.int32, (rows, rows), 1)
+    factor = HD**-0.5 * LOG2E
+    outgoing = [
+        pltpu.make_async_remote_copy(
+            src_ref=o_s.at[i],
+            dst_ref=back_s.at[slot],
+            send_sem=out_sem.at[0, i],
+            recv_sem=out_sem.at[1, slot],
+            device_id={"ctx": i},
+            device_id_type=pl.DeviceIdType.MESH,
+        )
+        for i in range(group)
+    ]
+    incoming = [
+        pltpu.make_async_remote_copy(
+            src_ref=o_s.at[i],
+            dst_ref=back_s.at[i],
+            send_sem=out_sem.at[0, i],
+            recv_sem=out_sem.at[1, i],
+            device_id={"ctx": i},
+            device_id_type=pl.DeviceIdType.MESH,
+        )
+        for i in range(group)
+    ]
+    for i in range(group):
+        q = got_s[i, 0]
+        keys = got_s[: i + 1, 1].reshape((i + 1) * rows, HD)
+        values = got_s[: i + 1, 2].reshape((i + 1) * rows, HD)
+        s = lax.dot_general(
+            q, keys, (((1,), (1,)), ((), ())), preferred_element_type=jnp.float32
+        )
+        last = jnp.where(col <= row, s[:, i * rows :], -jnp.inf)
+        s = jnp.concatenate([s[:, : i * rows], last], axis=1) if i else last
+        top = jnp.max(s, axis=1, keepdims=True)
+        p = jnp.exp2((s - top) * factor)
+        o = jnp.dot(p.astype(jnp.bfloat16), values, preferred_element_type=jnp.float32)
+        o_s[i] = (o / jnp.sum(p, axis=1, keepdims=True)).astype(jnp.bfloat16)
+        pl.when(slot != i)(outgoing[i].start)
+
+
+    @pl.when(slot >= half)
+    def _():
+        first_copies[0].wait_recv()
+        for n in range(NS):
+            inc_s[tile[n], :] = (
+                jnp.exp2(inc_s[tile[NS], :] * a_ref[tile[n], :]) * first_s[tile[n], :]
+                + inc_s[tile[n], :]
+            )
 
     def correct(block, carry):
         held = list(carry)
@@ -429,11 +479,21 @@
         mix_ref[:, cols] = (y * (g / (1.0 + jnp.exp(-g)))).astype(mix_ref.dtype)
 
     att_ref[:, pl.ds(pl.multiple_of(slot * HD, HD), HD)] = o_s[slot]
-    for d in range(1, group):
-        out_copies[d - 1].wait()
-        att_ref[:, pl.ds(pl.multiple_of(origin[d] * HD, HD), HD)] = back_s[d - 1]
-    for d in range(1, group):
-        pl.when(slot + d < group)(end_copies[d - 1].wait_send)
+    for i in range(group):
+
+        @pl.when(slot != i)
+        def _(i=i):
+            outgoing[i].wait_send()
+            incoming[i].wait_recv()
+            att_ref[:, i * HD : (i + 1) * HD] = back_s[i]
+
+    for d in range(1, half):
+        pl.when(place + d < half)(end_copies[d - 1].wait_send)
+
+    @pl.when(slot == half - 1)
+    def _():
+        for copy in first_copies:
+            copy.wait_send()
 
 
 def whole(query, key, value, xin, gate_z, delta, part, rate2, skip):
@@ -457,14 +517,17 @@
             tiles,
             tiles,
             pltpu.VMEM(ends, f32),
-            pltpu.VMEM((group - 1, *ends), f32),
+            pltpu.VMEM((group // 2 - 1, *ends), f32),
+            pltpu.VMEM(ends, f32),
+            pltpu.VMEM((NS * SUB, LANES), f32),
             pltpu.VMEM((NS * SUB, LANES), f32),
             pltpu.VMEM((group, rows, HD), bf16),
-            pltpu.VMEM((group - 1, rows, HD), bf16),
+            pltpu.VMEM((group, rows, HD), bf16),
             pltpu.SemaphoreType.DMA((2, tp - 1)),
             pltpu.SemaphoreType.DMA((2, group - 1)),
-            pltpu.SemaphoreType.DMA((2, group - 1)),
-            pltpu.SemaphoreType.DMA((2, group - 1)),
+            pltpu.SemaphoreType.DMA((2, group // 2 - 1)),
+            pltpu.SemaphoreType.DMA((1 + group // 2,)),
+            pltpu.SemaphoreType.DMA((2, group)),
             pltpu.SemaphoreType.DMA,
         ],
         compiler_params=pltpu.CompilerParams(

time: 71.3 us -> 64.3 us (0.902)
  the two profiles are of different devices: /device:TPU:0 before, /device:TPU:26 now
where the time goes in v3:
time: 64.3 us; the launch traced here: 64.1 us
  Pallas kernels  57.9 us (90%)
  local copies, waits for them, and re-layouts  3.36 us (5%)
  matrix products  2.15 us (3%)
  between operations  0.76 us (1%)
    pallas_call x1, Pallas kernels, whole(): pl.pallas_call(functools.partial(whole_kernel, group, tp), out_shape=[jax...  57.9 us
    unnamed x22, local copies, waits for them, and re-layouts  3.34 us
    dot_general x1, matrix products, shards(): lax.dot_general(w_bc, xin, (((0,), (1,)), ((), ())), preferred_element_ty...  1.4 us

profile of v3, /device:TPU:26, one launch (start us, length us, event | category | flops | bytes accessed | tf_op | source)
XLA Modules:
  0.0 64.1 jit_solution(11053354835530243994)
XLA Ops:
  0.6 0.0 copy-start
  0.6 0.0 copy-start.7
  0.7 1.4 %fusion.refs_6_ = f32[32,256]{1,0:T(8,128)S(1)} fusion(bf16[1024,32]{0,1:T(8,128)(2,1)} %param.16, bf16[256,1024]{1,0:T(8,128)(2,1)} %refs_3_.1), kind=kOutput, calls=%fused_computation.3 | convolution fusion | flops 16777216 | bytes 622592 | tf_op jit(solution)/shard_map/dot_general | solution.py:549
  2.1 0.0 copy-done.7
  2.1 0.0 copy-start.8
  2.1 0.0 copy-start.9
  2.1 0.0 copy-done
  2.2 0.8 %copy-done.8 = bf16[256,256]{1,0:T(8,128)(2,1)S(1)} copy-done((bf16[256,256]{1,0:T(8,128)(2,1)S(1)}, bf16[256,256]{1,0:T(8,128)(2,1)}, u32[]{:S(2)}) %copy-start.8) | copy-done | bytes 131096
  3.0 0.0 copy-done.9
  3.0 0.0 copy-start.1
  3.0 0.0 copy-start.2
  3.0 0.0 copy-start.4
  3.0 0.0 copy-start.5
  3.0 0.0 copy-start.6
  3.0 0.8 %compare_select_fusion.refs_5_ = f32[256,1024]{1,0:T(8,128)S(1)} fusion(bf16[256,256]{1,0:T(8,128)(2,1)S(1)} %copy-done.8, bf16[256,1024]{1,0:T(8,128)(2,1)S(1)} %copy-done, f32[1024]{0:T(1024)S(1)} %copy-done.9), kind=kOutput, calls=%fused_computation | convolution fusion | flops 136052736 | bytes 1708032 | tf_op jit(solution)/shard_map/dot_general | solution.py:545
  3.8 0.2 copy-done.1
  4.0 0.2 copy-done.2
  4.2 0.2 copy-done.3
  4.3 0.2 copy-done.4
  4.5 0.2 copy-done.5
  4.7 0.0 copy-done.6
  4.7 57.9 %shard_map.122 = (bf16[256,1024]{1,0:T(8,128)(2,1)S(1)}, bf16[256,1024]{1,0:T(8,128)(2,1)S(1)}) custom-call(bf16[256,1024]{1,0:T(8,128)(2,1)S(1)} %copy-done.2, bf16[256,1024]{1,0:T(8,128)(2,1)S(1)} %copy-done.3, bf16[256,1024]{1,0:T(8,128)(2,1)S(1)} %copy-done.4, bf16[256,1024]{1,0:T(8,128)(2,1)S(1)} %copy-done.1, bf16[256,1024]{1,0:T(8,128)(2,1)S(1)} %copy-done.5, ...), custom_call_target="tpu_custom_call" | custom-call | tf_op jit(solution)/shard_map/pallas_call | solution.py:505
  62.5 0.8 %copy.15 = bf16[256,1024]{1,0:T(8,128)(2,1)} copy(bf16[256,1024]{1,0:T(8,128)(2,1)S(1)} %get-tuple-element.4) | data formatting | bytes 1048576
  63.3 0.8 %copy.16 = bf16[256,1024]{1,0:T(8,128)(2,1)} copy(bf16[256,1024]{1,0:T(8,128)(2,1)S(1)} %get-tuple-element.5) | data formatting | bytes 1048576
  (3 shorter events, 0.0 us)
Async XLA Ops:
  0.6 1.5 %copy-start = (bf16[256,1024]{1,0:T(8,128)(2,1)S(1)}, bf16[256,1024]{1,0:T(8,128)(2,1)}, u32[]{:S(2)}) copy-start(bf16[256,1024]{1,0:T(8,128)(2,1)} %param.18) | copy-start | bytes 1572868
  0.6 1.4 %copy-start.7 = (f32[16,1024]{1,0:T(8,128)S(1)}, f32[16,1024]{1,0:T(8,128)}, u32[]{:S(2)}) copy-start(f32[16,1024]{1,0:T(8,128)} %param.20) | copy-start | bytes 196612
  2.1 0.9 %copy-start.8 = (bf16[256,256]{1,0:T(8,128)(2,1)S(1)}, bf16[256,256]{1,0:T(8,128)(2,1)}, u32[]{:S(2)}) copy-start(bf16[256,256]{1,0:T(8,128)(2,1)} %param.17) | copy-start | bytes 393220
  2.1 0.9 %copy-start.9 = (f32[1024]{0:T(1024)S(1)}, f32[1024]{0:T(1024)}, u32[]{:S(2)}) copy-start(f32[1024]{0:T(1024)} %param.19) | copy-start | bytes 12292
  3.0 1.0 %copy-start.1 = (bf16[256,1024]{1,0:T(8,128)(2,1)S(1)}, bf16[256,1024]{1,0:T(8,128)(2,1)}, u32[]{:S(2)}) copy-start(bf16[256,1024]{1,0:T(8,128)(2,1)} %refs_3_.1) | copy-start | bytes 1572868
  3.0 1.2 %copy-start.2 = (bf16[256,1024]{1,0:T(8,128)(2,1)S(1)}, bf16[256,1024]{1,0:T(8,128)(2,1)}, u32[]{:S(2)}) copy-start(bf16[256,1024]{1,0:T(8,128)(2,1)} %refs_0_.1) | copy-start | bytes 1572868
  3.0 1.4 %copy-start.3 = (bf16[256,1024]{1,0:T(8,128)(2,1)S(1)}, bf16[256,1024]{1,0:T(8,128)(2,1)}, u32[]{:S(2)}) copy-start(bf16[256,1024]{1,0:T(8,128)(2,1)} %refs_1_.1) | copy-start | bytes 1572868
  3.0 1.5 %copy-start.4 = (bf16[256,1024]{1,0:T(8,128)(2,1)S(1)}, bf16[256,1024]{1,0:T(8,128)(2,1)}, u32[]{:S(2)}) copy-start(bf16[256,1024]{1,0:T(8,128)(2,1)} %refs_2_.1) | copy-start | bytes 1572868
  3.0 1.7 %copy-start.5 = (bf16[256,1024]{1,0:T(8,128)(2,1)S(1)}, bf16[256,1024]{1,0:T(8,128)(2,1)}, u32[]{:S(2)}) copy-start(bf16[256,1024]{1,0:T(8,128)(2,1)} %refs_4_.1) | copy-start | bytes 1572868
  3.0 1.6 %copy-start.6 = (f32[1024]{0:T(1024)S(1)}, f32[1024]{0:T(1024)}, u32[]{:S(2)}) copy-start(f32[1024]{0:T(1024)} %param.21) | copy-start | bytes 12292

commit v4 on v3

--- a/solution.py
+++ b/solution.py
@@ -16,6 +16,7 @@
 LOG2E = math.log2(math.e)
 RADIX = 8
 VMEM = pl.BlockSpec(memory_space=pltpu.VMEM)
+HBM = pl.BlockSpec(memory_space=pltpu.HBM)
 SMEM = pl.BlockSpec(memory_space=pltpu.SMEM)
 PARAMS = pltpu.CompilerParams(vmem_limit_bytes=40 * 1024 * 1024)
 
@@ -280,10 +281,12 @@
 
 
 def whole_kernel(group, tp, *refs):
-    q_ref, k_ref, v_ref, x_ref, gate_ref, delta_ref, part_ref, a_ref, skip_ref = refs[:9]
-    att_ref, mix_ref = refs[9:11]
-    (pack_s, got_s, bcs_s, bc_v, bc_s, y_s, d_s, u_s, end_s, ends_s, inc_s, all_s, first_s, o_s, back_s) = refs[11:26]
-    bc_sem, qkv_sem, end_sem, first_sem, out_sem, copy_sem = refs[26:]
+    q_ref, k_ref, v_ref, x_hbm, gate_hbm, proj_hbm, low_ref, w_ref, bias_ref, a_ref, skip_ref = refs[:11]
+    att_ref, mix_ref = refs[11:13]
+    x_ref, gate_ref, proj_ref, part_ref = refs[13:17]
+    (pack_s, got_s, bcs_s, bc_v, bc_s, y_s, d_s, u_s, end_s, ends_s) = refs[17:27]
+    inc_s, all_s, first_s, o_s, back_s = refs[27:32]
+    bc_sem, qkv_sem, end_sem, first_sem, out_sem, copy_sem, load_sem, side_sem = refs[32:]
     rows = x_ref.shape[0]
     slot = lax.axis_index("ctx")
     line = lax.axis_index("tp")
@@ -301,31 +304,75 @@
             device_id={"tp": lax.rem(line + d, tp)},
             device_id_type=pl.DeviceIdType.MESH,
         )
+    loads = []
+    for d in (*range(1, group), 0):
+        col = pl.ds(pl.multiple_of(peer[d] * HD, HD), HD)
+        room = pack_s.at[d - 1] if d else got_s.at[slot]
+        for part, ref in enumerate((q_ref, k_ref, v_ref)):
+            loads.append(
+                pltpu.make_async_copy(ref.at[:, col], room.at[part], load_sem.at[d, part])
+            )
+    sides = [
+        pltpu.make_async_copy(src, dst, side_sem.at[k])
+        for k, (src, dst) in enumerate(
+            ((x_hbm, x_ref), (proj_hbm, proj_ref), (gate_hbm, gate_ref))
+        )
+    ]
+    for copy in loads[:3] + sides[:1] + loads[3:] + sides[1:]:
+        copy.start()
+    pl.semaphore_wait(barrier, group + tp - 2)
+
+    qkv_out = [
+        pltpu.make_async_remote_copy(
+            src_ref=pack_s.at[d - 1],
+            dst_ref=got_s.at[slot],
+            send_sem=qkv_sem.at[0, d],
+            recv_sem=qkv_sem.at[1, slot],
+            device_id={"ctx": peer[d]},
+            device_id_type=pl.DeviceIdType.MESH,
+        )
+        for d in range(1, group)
+    ]
+    qkv_in = [
+        pltpu.make_async_remote_copy(
+            src_ref=pack_s.at[0],
+            dst_ref=got_s.at[i],
+            send_sem=qkv_sem.at[0, 1],
+            recv_sem=qkv_sem.at[1, i],
+            device_id={"ctx": peer[1]},
+            device_id_type=pl.DeviceIdType.MESH,
+        )
+        for i in range(group)
+    ]
     for d in range(1, group):
-        col = pl.ds(pl.multiple_of(peer[d] * HD, HD), HD)
-        for part, ref in enumerate((q_ref, k_ref, v_ref)):
-            pack_s[d - 1, part] = ref[:, col]
-    col = pl.ds(pl.multiple_of(slot * HD, HD), HD)
-    for part, ref in enumerate((q_ref, k_ref, v_ref)):
-        got_s[slot, part] = ref[:, col]
-    pl.semaphore_wait(barrier, group + tp - 2)
-
+        for copy in loads[3 * d - 3 : 3 * d]:
+            copy.wait()
+        qkv_out[d - 1].start()
+    sides[0].wait()
+    part_ref[...] = lax.dot_general(
+        w_ref[...], x_ref[...], (((1,), (1,)), ((), ())), preferred_element_type=jnp.float32
+    )
     bc_copies = [
         send(part_ref, bcs_s.at[d - 1], bc_sem, d - 1, "tp", lax.rem(line + d, tp))
         for d in range(1, tp)
     ]
     for copy in bc_copies:
         copy.start()
-    qkv_copies = [
-        send(pack_s.at[d - 1], got_s.at[slot], qkv_sem, d - 1, "ctx", peer[d])
-        for d in range(1, group)
-    ]
-    for copy in qkv_copies:
-        copy.start()
+    for copy in loads[3 * group - 3 :]:
+        copy.wait()
+    sides[1].wait()
 
     for c in range(SUB):
         cols = slice(c * LANES, (c + 1) * LANES)
-        dt = delta_ref[:, cols]
+        raw = bias_ref[:, cols] + jnp.dot(
+            low_ref[...], proj_ref[:, cols], preferred_element_type=jnp.float32
+        )
+        z = jnp.exp(-jnp.abs(raw))
+        w = 1.0 + z
+        tiny = w == 1.0
+        dt = jnp.maximum(raw, 0.0) + jnp.where(
+            tiny, z, jnp.log(w) * (z / jnp.where(tiny, 1.0, w - 1.0))
+        )
         d_s[pl.ds(c, rows, stride=SUB), :] = dt
         u_s[pl.ds(c, rows, stride=SUB), :] = dt * x_ref[:, cols].astype(jnp.float32)
     total = part_ref[...]
@@ -369,44 +416,6 @@
     for d in range(1, half):
         pl.when(place + d < half)(end_copies[d - 1].start)
 
-    for copy in qkv_copies:
-        copy.wait()
-    inc_s[...] = jnp.zeros_like(inc_s)
-    for d in range(half - 1, 0, -1):
-
-        @pl.when(place >= d)
-        def _(d=d):
-            end_copies[d - 1].wait_recv()
-            through = ends_s[d - 1, tile[NS], :]
-            for n in range(NS):
-                inc_s[tile[n], :] = (
-                    jnp.exp2(through * a_ref[tile[n], :]) * inc_s[tile[n], :]
-                    + ends_s[d - 1, tile[n], :]
-                )
-            inc_s[tile[NS], :] = inc_s[tile[NS], :] + through
-
-    first_copies = [
-        pltpu.make_async_remote_copy(
-            src_ref=all_s,
-            dst_ref=first_s,
-            send_sem=first_sem.at[1 + k],
-            recv_sem=first_sem.at[0],
-            device_id={"ctx": half + k},
-            device_id_type=pl.DeviceIdType.MESH,
-        )
-        for k in range(group - half)
-    ]
-
-    @pl.when(slot == half - 1)
-    def _():
-        through = end_s[tile[NS], :]
-        for n in range(NS):
-            all_s[tile[n], :] = (
-                jnp.exp2(through * a_ref[tile[n], :]) * inc_s[tile[n], :] + end_s[tile[n], :]
-            )
-        for copy in first_copies:
-            copy.start()
-
     row = lax.broadcasted_iota(jnp.int32, (rows, rows), 0)
     col = lax.broadcasted_iota(jnp.int32, (rows, rows), 1)
     factor = HD**-0.5 * LOG2E
@@ -433,6 +442,7 @@
         for i in range(group)
     ]
     for i in range(group):
+        pl.when(slot != i)(qkv_in[i].wait_recv)
         q = got_s[i, 0]
         keys = got_s[: i + 1, 1].reshape((i + 1) * rows, HD)
         values = got_s[: i + 1, 2].reshape((i + 1) * rows, HD)
@@ -446,7 +456,42 @@
         o = jnp.dot(p.astype(jnp.bfloat16), values, preferred_element_type=jnp.float32)
         o_s[i] = (o / jnp.sum(p, axis=1, keepdims=True)).astype(jnp.bfloat16)
         pl.when(slot != i)(outgoing[i].start)
-
+        if i == half - 1:
+            inc_s[...] = jnp.zeros_like(inc_s)
+            for d in range(half - 1, 0, -1):
+
+                @pl.when(place >= d)
+                def _(d=d):
+                    end_copies[d - 1].wait_recv()
+                    through = ends_s[d - 1, tile[NS], :]
+                    for n in range(NS):
+                        inc_s[tile[n], :] = (
+                            jnp.exp2(through * a_ref[tile[n], :]) * inc_s[tile[n], :]
+                            + ends_s[d - 1, tile[n], :]
+                        )
+                    inc_s[tile[NS], :] = inc_s[tile[NS], :] + through
+
+            first_copies = [
+                pltpu.make_async_remote_copy(
+                    src_ref=all_s,
+                    dst_ref=first_s,
+                    send_sem=first_sem.at[1 + k],
+                    recv_sem=first_sem.at[0],
+                    device_id={"ctx": half + k},
+                    device_id_type=pl.DeviceIdType.MESH,
+                )
+                for k in range(group - half)
+            ]
+
+            @pl.when(slot == half - 1)
+            def _():
+                through = end_s[tile[NS], :]
+                for n in range(NS):
+                    all_s[tile[n], :] = (
+                        jnp.exp2(through * a_ref[tile[n], :]) * inc_s[tile[n], :] + end_s[tile[n], :]
+                    )
+                for copy in first_copies:
+                    copy.start()
 
     @pl.when(slot >= half)
     def _():
@@ -472,6 +517,7 @@
         return tuple(held)
 
     lax.fori_loop(0, rows // per, correct, tuple(inc_s[tile[n], :] for n in range(NS)))
+    sides[2].wait()
     for c in range(SUB):
         cols = slice(c * LANES, (c + 1) * LANES)
         y = y_s[pl.ds(c, rows, stride=SUB), :] + skip_ref[:, cols] * x_ref[:, cols].astype(jnp.float32)
@@ -487,6 +533,8 @@
             incoming[i].wait_recv()
             att_ref[:, i * HD : (i + 1) * HD] = back_s[i]
 
+    for copy in qkv_out:
+        copy.wait_send()
     for d in range(1, half):
         pl.when(place + d < half)(end_copies[d - 1].wait_send)
 
@@ -496,7 +544,7 @@
             copy.wait_send()
 
 
-def whole(query, key, value, xin, gate_z, delta, part, rate2, skip):
+def whole(query, key, value, xin, gate_z, dt_proj, dt_low, w_rows, dt_bias, rate2, skip):
     rows, channels = xin.shape
     group, tp = lax.axis_size("ctx"), lax.axis_size("tp")
     f32, bf16 = jnp.float32, jnp.bfloat16
@@ -505,9 +553,13 @@
     return pl.pallas_call(
         functools.partial(whole_kernel, group, tp),
         out_shape=[jax.ShapeDtypeStruct((rows, channels), bf16)] * 2,
-        in_specs=[VMEM] * 9,
+        in_specs=[HBM] * 6 + [VMEM] * 5,
         out_specs=[VMEM] * 2,
         scratch_shapes=[
+            pltpu.VMEM((rows, channels), bf16),
+            pltpu.VMEM((rows, channels), bf16),
+            pltpu.VMEM(dt_proj.shape, bf16),
+            pltpu.VMEM((2 * NS, rows), f32),
             pltpu.VMEM((group - 1, 3, rows, HD), bf16),
             pltpu.VMEM((group, 3, rows, HD), bf16),
             pltpu.VMEM((tp - 1, 2 * NS, rows), f32),
@@ -524,16 +576,18 @@
             pltpu.VMEM((group, rows, HD), bf16),
             pltpu.VMEM((group, rows, HD), bf16),
             pltpu.SemaphoreType.DMA((2, tp - 1)),
-            pltpu.SemaphoreType.DMA((2, group - 1)),
+            pltpu.SemaphoreType.DMA((2, group)),
             pltpu.SemaphoreType.DMA((2, group // 2 - 1)),
             pltpu.SemaphoreType.DMA((1 + group // 2,)),
             pltpu.SemaphoreType.DMA((2, group)),
             pltpu.SemaphoreType.DMA,
+            pltpu.SemaphoreType.DMA((group, 3)),
+            pltpu.SemaphoreType.DMA((3,)),
         ],
         compiler_params=pltpu.CompilerParams(
-            collective_id=0, has_side_effects=True, vmem_limit_bytes=40 * 1024 * 1024
+            collective_id=0, has_side_effects=True, vmem_limit_bytes=60 * 1024 * 1024
         ),
-    )(query, key, value, xin, gate_z, delta, part, rate2, skip)
+    )(query, key, value, xin, gate_z, dt_proj, dt_low, w_rows, dt_bias, rate2, skip)
 
 
 def shards(query, key, value, xin, gate_z, w_bc, dt_low, dt_proj, dt_bias, a_rate, skip):
@@ -541,15 +595,17 @@
     group = query.shape[1] // HD
     assert group * rows == WINDOW and lax.axis_size("ctx") % group == 0
     assert channels == SUB * LANES
+    rate2 = (a_rate * -LOG2E).reshape(NS * SUB, LANES)
+    if lax.axis_size("ctx") == group:
+        return tuple(
+            whole(
+                query, key, value, xin, gate_z, dt_proj, dt_low, w_bc.T, dt_bias[None, :], rate2,
+                skip[None, :],
+            )
+        )
     delta = jax.nn.softplus(
         jnp.dot(dt_low, dt_proj, preferred_element_type=jnp.float32) + dt_bias[None, :]
     )
-    rate2 = (a_rate * -LOG2E).reshape(NS * SUB, LANES)
-    if lax.axis_size("ctx") == group:
-        part = lax.dot_general(
-            w_bc, xin, (((0,), (1,)), ((), ())), preferred_element_type=jnp.float32
-        )
-        return tuple(whole(query, key, value, xin, gate_z, delta, part, rate2, skip[None, :]))
     packed = pack(query, key, value, group)
     partial_bc = jnp.dot(xin, w_bc, preferred_element_type=jnp.float32)
     tp = lax.axis_size("tp")

time: 64.3 us -> 62.2 us (0.967)
  the two profiles are of different devices: /device:TPU:26 before, /device:TPU:28 now
where the time goes in v4:
time: 62.2 us; the launch traced here: 62 us
  Pallas kernels  57.1 us (92%)
  local copies, waits for them, and re-layouts  3.37 us (5%)
  other arithmetic  0.85 us (1%)
  between operations  0.65 us (1%)
    pallas_call x1, Pallas kernels, whole(): pl.pallas_call(functools.partial(whole_kernel, group, tp), out_shape=[jax...  57.1 us
    unnamed x4, local copies, waits for them, and re-layouts  2.72 us

profile of v4, /device:TPU:28, one launch (start us, length us, event | category | flops | bytes accessed | tf_op | source)
XLA Modules:
  0.0 62.0 jit_solution(5522967250587319118)
XLA Ops:
  0.6 0.8 %broadcast_multiply_fusion = f32[16,1024]{1,0:T(8,128)S(1)} fusion(f32[16,1024]{1,0:T(8,128)} %param.20), kind=kLoop, calls=%fused_computation | loop fusion | flops 16384 | bytes 131072 | tf_op jit(solution)/shard_map/mul | solution.py:598
  1.5 0.6 %reshape.7.refs_9_ = f32[128,128]{1,0:T(8,128)} reshape(f32[16,1024]{1,0:T(8,128)S(1)} %broadcast_multiply_fusion) | data formatting | bytes 131072 | tf_op jit(solution)/shard_map/reshape | solution.py:598
  2.1 57.1 %shard_map.122 = (bf16[256,1024]{1,0:T(8,128)(2,1)}, bf16[256,1024]{1,0:T(8,128)(2,1)}) custom-call(bf16[256,1024]{1,0:T(8,128)(2,1)} %refs_0_.1, bf16[256,1024]{1,0:T(8,128)(2,1)} %refs_1_.1, bf16[256,1024]{1,0:T(8,128)(2,1)} %refs_2_.1, bf16[256,1024]{1,0:T(8,128)(2,1)} %refs_3_.1, bf16[256,1024]{1,0:T(8,128)(2,1)} %refs_4_.1, bf16[256,1024]{1,0:T(8,128)(2,1)} %refs_5_.1, ...), custom_call_target="tpu_custom_call" | custom-call | tf_op jit(solution)/shard_map/pallas_call | solution.py:553
  59.2 0.0 copy-start
  59.2 1.9 %copy.15 = bf16[256,1024]{1,0:T(8,128)(2,1)} copy(bf16[256,1024]{1,0:T(8,128)(2,1)} %get-tuple-element.4) | data formatting | bytes 1048576
  61.2 0.0 copy-done
  61.2 0.8 %copy.16 = bf16[256,1024]{1,0:T(8,128)(2,1)} copy(bf16[256,1024]{1,0:T(8,128)(2,1)S(1)} %copy-done) | data formatting | bytes 1048576
Async XLA Ops:
  59.2 1.9 %copy-start = (bf16[256,1024]{1,0:T(8,128)(2,1)S(1)}, bf16[256,1024]{1,0:T(8,128)(2,1)}, u32[]{:S(2)}) copy-start(bf16[256,1024]{1,0:T(8,128)(2,1)} %get-tuple-element.5) | copy-start | bytes 1572868
